TPU v7x, 32 devices: a whole 2x2x4 slice. The times are simulated.
32 devices in a mesh: dp: 16 (over z, x, core), mp: 2 (over y).
Axes of the slice: x: 2, y: 2, z: 4, core: 2. Of those that a mesh axis runs over, the one named last changes fastest.
Arguments:
- patches: bfloat16 [192, 196, 768], P(('dp', 'mp')), may hold values from -6 to 6
- cotangent: bfloat16 [192, 196, 768], P(('dp', 'mp')), may hold values from -26 to 26
- gain_one: float32 [768], replicated, may hold values from 0.5 to 2
- shift_one: float32 [768], replicated, may hold values from -3 to 3
- token_in: bfloat16 [196, 384], P(None, 'mp'), may hold values from -0.4375 to 0.4375
- token_bias: float32 [384], P('mp'), may hold values from -3 to 3
- token_out: bfloat16 [384, 196], P('mp'), may hold values from -0.4375 to 0.4375
- token_shift: float32 [196], replicated, may hold values from -3 to 3
- gain_two: float32 [768], replicated, may hold values from 0.5 to 2
- shift_two: float32 [768], replicated, may hold values from -3 to 3
- channel_in: bfloat16 [768, 3072], P(None, 'mp'), may hold values from -0.21875 to 0.21875
- channel_bias: float32 [3072], P('mp'), may hold values from -3 to 3
- channel_out: bfloat16 [3072, 768], P('mp'), may hold values from -0.15625 to 0.15625
- channel_shift: float32 [768], replicated, may hold values from -3 to 3
Outputs:
- mixed: bfloat16 [192, 196, 768], P(('dp', 'mp'))
- inputs_grad: float32 [192, 196, 768], P(('dp', 'mp'))
- gainone_grad: float32 [768], replicated
- shiftone_grad: float32 [768], replicated
- tokenin_grad: float32 [196, 384], P(None, 'mp')
- tokenbias_grad: float32 [384], P('mp')
- tokenout_grad: float32 [384, 196], P('mp')
- tokenshift_grad: float32 [196], replicated
- gaintwo_grad: float32 [768], replicated
- shifttwo_grad: float32 [768], replicated
- channelin_grad: float32 [768, 3072], P(None, 'mp')
- channelbias_grad: float32 [3072], P('mp')
- channelout_grad: float32 [3072, 768], P('mp')
- channelshift_grad: float32 [768], replicated
All inputs are finite; a program needn't handle non-finite values.
Results may differ from a plain program's by a relative error of at most 0.015.
Values may be sent and summed in bfloat16 or wider, within the bound.
A program may use at most 192 MiB of HBM per device.

v0:
```python
import jax
import jax.numpy as jnp
from jax import lax
from jax.sharding import PartitionSpec as P


def normalize(values, gain, shift):
    centred = values - jnp.mean(values, -1, keepdims=True)
    scale = lax.rsqrt(jnp.mean(centred * centred, -1, keepdims=True) + 1e-06)
    normed = centred * scale
    return (normed, scale, normed * gain + shift)


def norm_back(grad, normed, scale, gain):
    scaled = grad * gain
    return scale * (
        scaled
        - jnp.mean(scaled, -1, keepdims=True)
        - normed * jnp.mean(scaled * normed, -1, keepdims=True)
    )


def smooth(values):
    return jax.nn.gelu(values, approximate=False)


def smooth_back(values, grad):
    return jax.vjp(smooth, values)[1](grad)[0]


def per_device(
    patches,
    cotangent,
    gain_one,
    shift_one,
    token_in,
    token_bias,
    token_out,
    token_shift,
    gain_two,
    shift_two,
    channel_in,
    channel_bias,
    channel_out,
    channel_shift,
):
    width = patches.shape[2]
    resid = patches.astype(jnp.float32)
    normed_one, scale_one, affine_one = normalize(resid, gain_one, shift_one)
    mixer_rows = affine_one.astype(jnp.bfloat16)
    gathered_one = lax.all_gather(mixer_rows, "mp", axis=0, tiled=True)
    weights_in, bias_in, weights_out = (token_in, token_bias, token_out)
    token_pre = (
        jnp.einsum("bsd,sh->bhd", gathered_one, weights_in, preferred_element_type=jnp.float32)
        + bias_in[None, :, None]
    )
    token_hidden = smooth(token_pre).astype(jnp.bfloat16)
    token_part = jnp.einsum(
        "bhd,hs->bsd", token_hidden, weights_out, preferred_element_type=jnp.float32
    )
    token_sum = lax.psum_scatter(
        token_part.astype(jnp.bfloat16), "mp", scatter_dimension=0, tiled=True
    ).astype(jnp.float32)
    middle = resid + token_sum + token_shift[None, :, None]
    normed_two, scale_two, affine_two = normalize(middle, gain_two, shift_two)
    gathered_two = lax.all_gather(affine_two.astype(jnp.bfloat16), "mp", axis=0, tiled=True)
    mat_in, vec_bias, mat_out = (channel_in, channel_bias, channel_out)
    rows_two = gathered_two.reshape(-1, width)
    channel_pre = jnp.dot(rows_two, mat_in, preferred_element_type=jnp.float32) + vec_bias
    channel_hidden = smooth(channel_pre).astype(jnp.bfloat16)
    channel_part = jnp.dot(channel_hidden, mat_out, preferred_element_type=jnp.float32).reshape(
        gathered_two.shape
    )
    channel_sum = lax.psum_scatter(
        channel_part.astype(jnp.bfloat16), "mp", scatter_dimension=0, tiled=True
    ).astype(jnp.float32)
    mixed = (middle + channel_sum + channel_shift).astype(jnp.bfloat16)
    upstream = cotangent.astype(jnp.float32)
    grad_rows = lax.all_gather(cotangent, "mp", axis=0, tiled=True).reshape(-1, width)
    pre_again = (
        jnp.dot(lax.optimization_barrier(rows_two), mat_in, preferred_element_type=jnp.float32)
        + vec_bias
    )
    hidden_again = smooth(pre_again).astype(jnp.bfloat16)
    channelout_grad = jnp.einsum(
        "rh,rd->hd", hidden_again, grad_rows, preferred_element_type=jnp.float32
    )
    hidden_grad = jnp.einsum("rd,hd->rh", grad_rows, mat_out, preferred_element_type=jnp.float32)
    pre_grad = smooth_back(pre_again, hidden_grad).astype(jnp.bfloat16)
    channelbias_grad = jnp.sum(pre_grad.astype(jnp.float32), 0)
    channelin_grad = jnp.einsum("rd,rh->dh", rows_two, pre_grad, preferred_element_type=jnp.float32)
    second_part = jnp.einsum(
        "rh,dh->rd", pre_grad, mat_in, preferred_element_type=jnp.float32
    ).reshape(gathered_two.shape)
    second_grad = lax.psum_scatter(
        second_part.astype(jnp.bfloat16), "mp", scatter_dimension=0, tiled=True
    ).astype(jnp.float32)
    gaintwo_grad = jnp.sum(second_grad * normed_two, (0, 1))
    shifttwo_grad = jnp.sum(second_grad, (0, 1))
    middle_grad = upstream + norm_back(second_grad, normed_two, scale_two, gain_two)
    branch_grad = middle_grad.astype(jnp.bfloat16)
    tokenshift_grad = jnp.sum(branch_grad.astype(jnp.float32), (0, 2))
    channelshift_grad = jnp.sum(upstream, (0, 1))
    gathered_grad = lax.all_gather(branch_grad, "mp", axis=0, tiled=True)
    tokenout_grad = jnp.einsum(
        "bhd,bsd->hs", token_hidden, gathered_grad, preferred_element_type=jnp.float32
    )
    token_hidden_grad = jnp.einsum(
        "bsd,hs->bhd", gathered_grad, weights_out, preferred_element_type=jnp.float32
    )
    token_pre_grad = smooth_back(token_pre, token_hidden_grad).astype(jnp.bfloat16)
    tokenbias_grad = jnp.sum(token_pre_grad.astype(jnp.float32), (0, 2))
    tokenin_grad = jnp.einsum(
        "bsd,bhd->sh", gathered_one, token_pre_grad, preferred_element_type=jnp.float32
    )
    first_part = jnp.einsum(
        "bhd,sh->bsd", token_pre_grad, weights_in, preferred_element_type=jnp.float32
    )
    first_grad = lax.psum_scatter(
        first_part.astype(jnp.bfloat16), "mp", scatter_dimension=0, tiled=True
    ).astype(jnp.float32)
    inputs_grad = middle_grad + norm_back(first_grad, normed_one, scale_one, gain_one)
    gainone_grad = jnp.sum(first_grad * normed_one, (0, 1))
    shiftone_grad = jnp.sum(first_grad, (0, 1))
    summed = lax.psum(
        (
            tokenin_grad,
            tokenbias_grad,
            tokenout_grad,
            channelin_grad,
            channelbias_grad,
            channelout_grad,
        ),
        "dp",
    )
    shared = lax.psum(
        (
            gainone_grad,
            shiftone_grad,
            tokenshift_grad,
            gaintwo_grad,
            shifttwo_grad,
            channelshift_grad,
        ),
        ("dp", "mp"),
    )
    return (
        mixed,
        inputs_grad,
        shared[0],
        shared[1],
        summed[0],
        summed[1],
        summed[2],
        shared[2],
        shared[3],
        shared[4],
        summed[3],
        summed[4],
        summed[5],
        shared[5],
    )


def solution(mesh):
    placed = (
        P(("dp", "mp"), None, None),
        P(("dp", "mp"), None, None),
        P(),
        P(),
        P(None, "mp"),
        P("mp"),
        P("mp", None),
        P(),
        P(),
        P(),
        P(None, "mp"),
        P("mp"),
        P("mp", None),
        P(),
    )
    return jax.shard_map(
        per_device,
        mesh=mesh,
        in_specs=placed,
        out_specs=(
            P(("dp", "mp"), None, None),
            P(("dp", "mp"), None, None),
            P(),
            P(),
            P(None, "mp"),
            P("mp"),
            P("mp", None),
            P(),
            P(),
            P(),
            P(None, "mp"),
            P("mp"),
            P("mp", None),
            P(),
        ),
        check_vma=False,
    )
```

profile of v0, /device:TPU:0, one launch (start us, length us, event | category | flops | bytes accessed | tf_op | source)
XLA Modules:
  0.0 772.1 jit_solution(17569610425527980832)
XLA Ops:
  9.3 2.2 fusion.88
  12.1 3.5 fusion.84
  15.6 53.8 %all-gather.5.cloned.1.call-done = bf16[12,196,768]{2,1,0:T(8,128)(2,1)} async-done(((bf16[6,196,768]{2,1,0:T(8,128)(2,1)}), bf16[12,196,768]{2,1,0:T(8,128)(2,1)}) %all-gather.5.cloned.1.call-update) | async-done | bytes 3612688 | tf_op jit(solution)/shard_map/all_gather | solution.py:51
  69.4 19.5 %fusion.59 = (bf16[12,192,768]{2,1,0:T(8,128)(2,1)S(1)}, f32[12,192,768]{2,1,0:T(8,128)}, f32[12,768,192]{1,2,0:T(8,128)}) fusion(f32[192]{0:T(256)S(1)} %copy-done.45, bf16[12,196,768]{2,1,0:T(8,128)(2,1)} %all-gather.5.cloned.1.call-done, bf16[196,192]{0,1:T(8,128)(2,1)S(1)} %copy-done.22), kind=kOutput, calls=%fused_computation.89 | convolution fusion | flops 810418176 | bytes 21383424 | tf_op jit(solution)/shard_map/bsd,sh->bhd/dot_general | solution.py:54
  90.9 3.1 convert_bitcast_fusion.1
  94.7 48.7 %reduce-scatter.5.cloned.1.call-done = bf16[6,196,768]{2,1,0:T(8,128)(2,1)} async-done(((bf16[12,196,768]{2,1,0:T(8,128)(2,1)}), bf16[6,196,768]{2,1,0:T(8,128)(2,1)}) %reduce-scatter.5.cloned.1.call-update) | async-done | bytes 1806352 | tf_op jit(solution)/shard_map/reduce_scatter | solution.py:61
  143.4 2.9 fusion.133
  146.3 3.1 multiply_reduce_fusion
  152.4 43.7 %all-gather.9.cloned.1.call-done = bf16[12,196,768]{2,1,0:T(8,128)(2,1)} async-done(((bf16[6,196,768]{2,1,0:T(8,128)(2,1)}), bf16[12,196,768]{2,1,0:T(8,128)(2,1)}) %all-gather.9.cloned.1.call-update) | async-done | bytes 3612688 | tf_op jit(solution)/shard_map/all_gather | solution.py:79
  196.1 5.7 reshape.87
  201.8 47.4 %all-gather.7.cloned.1.call-done = bf16[12,196,768]{2,1,0:T(8,128)(2,1)} async-done(((bf16[6,196,768]{2,1,0:T(8,128)(2,1)}), bf16[12,196,768]{2,1,0:T(8,128)(2,1)}) %all-gather.7.cloned.1.call-update) | async-done | bytes 3612688 | tf_op jit(solution)/shard_map/all_gather | solution.py:66
  249.2 5.7 reshape.86
  254.9 37.2 %fusion.3 = (f32[2352,1536]{1,0:T(8,128)}, f32[2352,1536]{1,0:T(8,128)}) fusion(f32[1536]{0:T(1024)S(1)} %copy-done.44, bf16[2352,768]{1,0:T(8,128)(2,1)} %reshape.86, bf16[768,1536]{1,0:T(8,128)(2,1)S(1)} %copy-done), kind=kOutput, calls=%fused_computation.5 | convolution fusion | flops 5776662528 | bytes 34879488 | tf_op jit(solution)/shard_map/dot_general | solution.py:81
  292.1 20.8 %convert_reduce_fusion = (f32[1536]{0:T(1024)}, bf16[2352,1536]{1,0:T(8,128)(2,1)}) fusion(f32[2352,1536]{1,0:T(8,128)} %get-tuple-element.42, f32[2352,1536]{1,0:T(8,128)} %get-tuple-element.43, bf16[2352,768]{1,0:T(8,128)(2,1)} %reshape.87, bf16[1536,768]{1,0:T(8,128)(2,1)} %param.26), kind=kOutput, calls=%fused_computation.7 | convolution fusion | flops 5606865408 | bytes 42104832 | tf_op jit(solution)/shard_map/rd,hd->rh/dot_general | solution.py:88
  312.9 10.3 %convolution_convert_fusion = bf16[2352,768]{1,0:T(8,128)(2,1)} fusion(bf16[2352,1536]{1,0:T(8,128)(2,1)} %get-tuple-element.47, bf16[768,1536]{1,0:T(8,128)(2,1)S(1)} %copy-done), kind=kOutput, calls=%fused_computation.119 | convolution fusion | flops 5550870528 | bytes 13197312 | tf_op jit(solution)/shard_map/rh,dh->rd/dot_general | solution.py:92
  323.2 5.7 convert_element_type.93
  329.5 48.9 %reduce-scatter.9.cloned.1.call-done = bf16[6,196,768]{2,1,0:T(8,128)(2,1)} async-done(((bf16[12,196,768]{2,1,0:T(8,128)(2,1)}), bf16[6,196,768]{2,1,0:T(8,128)(2,1)}) %reduce-scatter.9.cloned.1.call-update) | async-done | bytes 1806352 | tf_op jit(solution)/shard_map/reduce_scatter | solution.py:95
  378.5 4.6 fusion.94
  383.1 5.8 convert_reduce_fusion.6
  388.9 51.1 %all-gather.11.cloned.1.call-done = bf16[12,196,768]{2,1,0:T(8,128)(2,1)} async-done(((bf16[6,196,768]{2,1,0:T(8,128)(2,1)}), bf16[12,196,768]{2,1,0:T(8,128)(2,1)}) %all-gather.11.cloned.1.call-update) | async-done | bytes 3612688 | tf_op jit(solution)/shard_map/all_gather | solution.py:104
  440.1 10.6 %convert_reduce_fusion.1 = (f32[192]{0:T(256)}, bf16[12,192,768]{2,1,0:T(8,128)(2,1)S(1)}) fusion(f32[12,192,768]{2,1,0:T(8,128)} %get-tuple-element.37, bf16[12,196,768]{2,1,0:T(8,128)(2,1)} %all-gather.11.cloned.1.call-done, bf16[192,196]{1,0:T(8,128)(2,1)S(1)} %copy-done.21, f32[12,768,192]{1,2,0:T(8,128)} %get-tuple-element.41, f32[192]{0:T(256)S(1)} %copy-done.46), kind=kOutput, calls=%fused_computation.90 | convolution fusion | flops 723713856 | bytes 21384192 | tf_op jit(solution)/shard_map/bsd,hs->bhd/dot_general | solution.py:108
  452.4 3.0 convert_bitcast_fusion
  455.5 44.2 %fusion.78 = bf16[2352,768]{1,0:T(8,128)(2,1)} fusion(bf16[1536,768]{1,0:T(8,128)(2,1)} %param.26, bf16[2352,768]{1,0:T(8,128)(2,1)} %reshape.86, bf16[768,1536]{1,0:T(8,128)(2,1)S(1)} %copy-done, f32[1536]{0:T(1024)S(1)} %copy-done.44), kind=kOutput, calls=%fused_computation.120 | convolution fusion | flops 11338371072 | bytes 11950080 | tf_op jit(solution)/shard_map/dot_general | solution.py:71
  499.7 5.7 convert_element_type.87
  505.5 11.3 %fusion.136 = f32[768,1536]{1,0:T(8,128)} fusion(bf16[2352,768]{1,0:T(8,128)(2,1)} %reshape.86, bf16[2352,1536]{1,0:T(8,128)(2,1)} %get-tuple-element.47), kind=kOutput, calls=%fused_computation.195 | convolution fusion | flops 5549064192 | bytes 15556608 | tf_op jit(solution)/shard_map/rd,rh->dh/dot_general | solution.py:91
  516.8 15.7 %fusion.17 = f32[1536,768]{1,0:T(8,128)} fusion(bf16[2352,768]{1,0:T(8,128)(2,1)S(1)} %copy-done.5, f32[2352,1536]{1,0:T(8,128)} %get-tuple-element.42, f32[2352,1536]{1,0:T(8,128)} %get-tuple-element.43), kind=kOutput, calls=%fused_computation.40 | convolution fusion | flops 5559902208 | bytes 37232640 | tf_op jit(solution)/shard_map/rh,rd->hd/dot_general | solution.py:85
  538.2 34.9 %all-reduce.1 = (f32[192]{0:T(256)}, f32[1536]{0:T(1024)}) all-reduce(f32[192]{0:T(256)S(1)} %copy-done.41, f32[1536]{0:T(1024)S(1)} %copy-done.37), channel_id=1, replica_groups=mesh['dp'=16,'mp'=2] {'dp'}, use_global_device_ids=true, to_apply=%region_18.0 | all-reduce | flops 1728 | bytes 13824 | tf_op jit(solution)/shard_map/psum | solution.py:125
  573.1 3.2 fusion.95
  576.4 8.5 %fusion.87 = (f32[6,196,768]{2,1,0:T(8,128)}, bf16[6,196,768]{2,1,0:T(8,128)(2,1)}, f32[768]{0:T(1024)S(1)}) fusion(bf16[6,196,768]{2,1,0:T(8,128)(2,1)S(1)} %copy-done.3, bf16[6,196,768]{2,1,0:T(8,128)(2,1)} %reduce-scatter.11.cloned.1.call-done, f32[6,196]{1,0:T(8,128)S(1)} %broadcast_multiply_fusion, f32[6,196]{1,0:T(8,128)S(1)} %broadcast_multiply_fusion.1, ...), kind=kLoop, calls=%fused_computation.131 | loop fusion | flops 25287936 | bytes 16307728 | tf_op jit(solution)/shard_map/add | solution.py:122
  584.9 39.1 %all-reduce = (f32[768]{0:T(1024)}, f32[768]{0:T(1024)}, f32[196]{0:T(256)}, f32[768]{0:T(1024)}, f32[768]{0:T(1024)}, /*index=5*/f32[768]{0:T(1024)}) all-reduce(f32[768]{0:T(1024)S(1)} %get-tuple-element.16, f32[768]{0:T(1024)S(1)} %get-tuple-element.21, f32[196]{0:T(256)S(1)} %copy-done.40, ...), channel_id=1, replica_groups=mesh['dp'=16,'mp'=2] {'dp','mp'}, use_global_device_ids=true, to_apply=%region_13.0 | all-reduce | flops 4036 | bytes 32288 | tf_op jit(solution)/shard_map/psum | solution.py:136
  624.0 130.6 %all-reduce.5.cloned.1.call-done = (f32[196,192]{0,1:T(8,128)}, f32[192,196]{1,0:T(8,128)}, f32[768,1536]{1,0:T(8,128)}, f32[1536,768]{1,0:T(8,128)}) async-done(((f32[196,192]{0,1:T(8,128)}, f32[192,196]{1,0:T(8,128)}, f32[768,1536]{1,0:T(8,128)}, f32[1536,768]{1,0:T(8,128)}), (f32[196,192]{0,1:T(8,128)}, f32[192,196]{1,0:T(8,128)}, f32[768,1536]{1,0:T(8,128)}, ...) | async-done | bytes 9738256 | tf_op jit(solution)/shard_map/psum | solution.py:125
  758.0 5.0 copy.34
  (133 shorter events, 22.1 us)
Async XLA Ops:
  7.2 247.7 %copy-start = (bf16[768,1536]{1,0:T(8,128)(2,1)S(1)}, bf16[768,1536]{1,0:T(8,128)(2,1)}, u32[]{:S(2)}) copy-start(bf16[768,1536]{1,0:T(8,128)(2,1)} %param.24) | copy-start | bytes 7077892
  7.2 62.2 %copy-start.45 = (f32[192]{0:T(256)S(1)}, f32[192]{0:T(256)}, u32[]{:S(2)}) copy-start(f32[192]{0:T(256)} %param.19) | copy-start | bytes 2308
  7.2 62.2 %copy-start.22 = (bf16[196,192]{0,1:T(8,128)(2,1)S(1)}, bf16[196,192]{0,1:T(8,128)(2,1)}, u32[]{:S(2)}) copy-start(bf16[196,192]{0,1:T(8,128)(2,1)} %param.18) | copy-start | bytes 225796
  7.2 62.2 %all-gather.5.cloned.1.call-start = ((), (), s32[]{:S(2)}) async-start(), calls=%async_computation.4 | async-start | bytes 5529600 | tf_op jit(solution)/shard_map/all_gather | solution.py:51
  15.6 75.3 %copy-start.20 = (bf16[192,196]{1,0:T(8,128)(2,1)S(1)}, bf16[192,196]{1,0:T(8,128)(2,1)}, u32[]{:S(2)}) copy-start(bf16[192,196]{1,0:T(8,128)(2,1)} %param.20) | copy-start | bytes 225796
  15.6 127.8 %reduce-scatter.5.cloned.1.call-start = ((), (), s32[]{:S(2)}) async-start(), calls=%async_computation.5 | async-start | bytes 5529600 | tf_op jit(solution)/shard_map/reduce_scatter | solution.py:61
  89.0 54.4 %copy-start.32 = (f32[196]{0:T(256)S(1)}, f32[196]{0:T(256)}, u32[]{:S(2)}) copy-start(f32[196]{0:T(256)} %param.21) | copy-start | bytes 2356
  93.9 56.1 %copy-start.28 = (f32[768]{0:T(1024)S(1)}, f32[768]{0:T(1024)}, u32[]{:S(2)}) copy-start(f32[768]{0:T(1024)} %param.22) | copy-start | bytes 9220
  93.9 56.1 %copy-start.38 = (f32[768]{0:T(1024)S(1)}, f32[768]{0:T(1024)}, u32[]{:S(2)}) copy-start(f32[768]{0:T(1024)} %param.23) | copy-start | bytes 9220
  94.0 102.1 %all-gather.9.cloned.1.call-start = ((), (), s32[]{:S(2)}) async-start(), calls=%async_computation.8 | async-start | bytes 5529600 | tf_op jit(solution)/shard_map/all_gather | solution.py:79
  94.7 154.5 %all-gather.7.cloned.1.call-start = ((), (), s32[]{:S(2)}) async-start(), calls=%async_computation.6 | async-start | bytes 5529600 | tf_op jit(solution)/shard_map/all_gather | solution.py:66
  152.1 102.8 %copy-start.44 = (f32[1536]{0:T(1024)S(1)}, f32[1536]{0:T(1024)}, u32[]{:S(2)}) copy-start(f32[1536]{0:T(1024)} %param.25) | copy-start | bytes 18436
  152.1 226.3 %reduce-scatter.9.cloned.1.call-start = ((), (), s32[]{:S(2)}) async-start(), calls=%async_computation.9 | async-start | bytes 5529600 | tf_op jit(solution)/shard_map/reduce_scatter | solution.py:95
  323.2 55.2 %copy-start.11 = (f32[6,196]{1,0:T(8,128)S(1)}, f32[6,196]{1,0:T(8,128)}, u32[]{:S(2)}) copy-start(f32[6,196]{1,0:T(8,128)} %copy-done.10) | copy-start | bytes 14116
  323.2 55.2 %copy-start.16 = (f32[6,196]{1,0:T(8,128)S(1)}, f32[6,196]{1,0:T(8,128)}, u32[]{:S(2)}) copy-start(f32[6,196]{1,0:T(8,128)} %copy-done.15) | copy-start | bytes 14116
  323.2 55.2 %copy-start.29 = (f32[768]{0:T(1024)S(1)}, f32[768]{0:T(1024)}, u32[]{:S(2)}) copy-start(f32[768]{0:T(1024)} %param.22) | copy-start | bytes 9220
  323.2 55.2 %copy-start.33 = (f32[196]{0:T(256)S(1)}, f32[196]{0:T(256)}, u32[]{:S(2)}) copy-start(f32[196]{0:T(256)} %param.21) | copy-start | bytes 2356
  329.0 111.1 %copy-start.21 = (bf16[192,196]{1,0:T(8,128)(2,1)S(1)}, bf16[192,196]{1,0:T(8,128)(2,1)}, u32[]{:S(2)}) copy-start(bf16[192,196]{1,0:T(8,128)(2,1)} %param.20) | copy-start | bytes 225796
  329.0 111.1 %copy-start.46 = (f32[192]{0:T(256)S(1)}, f32[192]{0:T(256)}, u32[]{:S(2)}) copy-start(f32[192]{0:T(256)} %param.19) | copy-start | bytes 2308
  329.0 111.0 %all-gather.11.cloned.1.call-start = ((), (), s32[]{:S(2)}) async-start(), calls=%async_computation.10 | async-start | bytes 5529600 | tf_op jit(solution)/shard_map/all_gather | solution.py:104
  388.9 184.2 %reduce-scatter.11.cloned.1.call-start = ((), (), s32[]{:S(2)}) async-start(), calls=%async_computation.11 | async-start | bytes 5529600 | tf_op jit(solution)/shard_map/reduce_scatter | solution.py:119
  455.5 120.9 %reduce-scatter.7.cloned.1.call-start = ((), (), s32[]{:S(2)}) async-start(), calls=%async_computation.7 | async-start | bytes 5529600 | tf_op jit(solution)/shard_map/reduce_scatter | solution.py:74
  505.4 249.2 %all-reduce.5.cloned.1.call-start = ((), (), s32[]{:S(2)}) async-start(), calls=%async_computation.12 | async-start | bytes 19660800 | tf_op jit(solution)/shard_map/psum | solution.py:125
  537.5 35.6 %copy-start.3 = (bf16[6,196,768]{2,1,0:T(8,128)(2,1)S(1)}, bf16[6,196,768]{2,1,0:T(8,128)(2,1)}, u32[]{:S(2)}) copy-start(bf16[6,196,768]{2,1,0:T(8,128)(2,1)} %param.14) | copy-start | bytes 5419012
  537.5 35.6 %copy-start.14 = (f32[6,196]{1,0:T(8,128)S(1)}, f32[6,196]{1,0:T(8,128)}, u32[]{:S(2)}) copy-start(f32[6,196]{1,0:T(8,128)} %copy-done.13) | copy-start | bytes 14116
  537.5 38.8 %copy-start.12 = (f32[6,196]{1,0:T(8,128)S(1)}, f32[6,196]{1,0:T(8,128)}, u32[]{:S(2)}) copy-start(f32[6,196]{1,0:T(8,128)} %copy-done.10) | copy-start | bytes 14116
  537.5 38.8 %copy-start.17 = (f32[6,196]{1,0:T(8,128)S(1)}, f32[6,196]{1,0:T(8,128)}, u32[]{:S(2)}) copy-start(f32[6,196]{1,0:T(8,128)} %copy-done.15) | copy-start | bytes 14116
  537.6 38.8 %copy-start.25 = (f32[6,196]{1,0:T(8,128)S(1)}, f32[6,196]{1,0:T(8,128)}, u32[]{:S(2)}) copy-start(f32[6,196]{1,0:T(8,128)} %copy-done.24) | copy-start | bytes 14116
  537.6 38.8 %copy-start.27 = (f32[6,196]{1,0:T(8,128)S(1)}, f32[6,196]{1,0:T(8,128)}, u32[]{:S(2)}) copy-start(f32[6,196]{1,0:T(8,128)} %copy-done.26) | copy-start | bytes 14116
  537.6 38.8 %copy-start.30 = (f32[768]{0:T(1024)S(1)}, f32[768]{0:T(1024)}, u32[]{:S(2)}) copy-start(f32[768]{0:T(1024)} %param.22) | copy-start | bytes 9220
  537.6 38.8 %copy-start.34 = (f32[196]{0:T(256)S(1)}, f32[196]{0:T(256)}, u32[]{:S(2)}) copy-start(f32[196]{0:T(256)} %param.21) | copy-start | bytes 2356
  537.6 38.8 %copy-start.39 = (f32[768]{0:T(1024)S(1)}, f32[768]{0:T(1024)}, u32[]{:S(2)}) copy-start(f32[768]{0:T(1024)} %param.27) | copy-start | bytes 9220
  (26 other events, 214.2 us)
Sparse Core Ops, SparseCore 0:
  15.7 53.7 all-gather.4
  94.1 49.2 reduce-scatter.4
  145.0 51.0 all-gather.8
  198.1 51.0 all-gather.6
  329.1 49.2 reduce-scatter.8
  389.0 51.0 all-gather.10
  455.6 49.2 reduce-scatter.10
  507.2 49.2 reduce-scatter.6
  561.8 192.8 all-reduce.4
where the time goes:
time: 780 us; the launch traced here: 772 us
  waiting for transfers between devices  425 us (54%)
  matrix products  179 us (23%)
  blocking collectives  73.9 us (9%)
  local copies, waits for them, and re-layouts  40.4 us (5%)
  other arithmetic  37.8 us (5%)
  between operations  14.6 us (2%)
    psum x1, waiting for transfers between devices, per_device(): lax.psum((tokenin_grad, tokenbias_grad, tokenout_grad, channelin_grad, ch...  131 us
    all_gather x1, waiting for transfers between devices, per_device(): gathered_one = lax.all_gather(mixer_rows, 'mp', axis=0, tiled=True)  53.8 us
    all_gather x1, waiting for transfers between devices, per_device(): gathered_grad = lax.all_gather(branch_grad, 'mp', axis=0, tiled=True)  51.1 us
    reduce_scatter x1, waiting for transfers between devices, per_device(): lax.psum_scatter(second_part.astype(jnp.bfloat16), 'mp', scatter_dimensio...  48.9 us
    reduce_scatter x1, waiting for transfers between devices, per_device(): lax.psum_scatter(token_part.astype(jnp.bfloat16), 'mp', scatter_dimension...  48.7 us
    all_gather x1, waiting for transfers between devices, per_device(): lax.all_gather(affine_two.astype(jnp.bfloat16), 'mp', axis=0, tiled=True)  47.4 us
    dot_general x1, matrix products, per_device(): jnp.dot(channel_hidden, mat_out, preferred_element_type=jnp.float32)  44.2 us
    all_gather x1, waiting for transfers between devices, per_device(): lax.all_gather(cotangent, 'mp', axis=0, tiled=True).reshape(-1, width)  43.7 us
  transfers between devices with their start and end apart: 9, of which 7 were waited for; matrix products, arithmetic and copies ran while one was open for 14% of the time, Pallas kernels for 0%

commit v1 on v0

v1 whole, which is shorter than its diff:
```python
import functools

import jax
import jax.numpy as jnp
from jax import lax
from jax.experimental import pallas as pl
from jax.experimental.pallas import tpu as pltpu
from jax.sharding import PartitionSpec as P

MESH = pl.DeviceIdType.MESH
F32 = jnp.float32
BF16 = jnp.bfloat16
NT = (((1,), (1,)), ((), ()))
LANES = 128
NUM, DEN = 7, 4
OFFSETS = (5, 8, 10, 12, 14, 15)


def dot(a, b):
    return jnp.dot(a, b, preferred_element_type=F32)


def dot_nt(a, b):
    return lax.dot_general(a, b, NT, preferred_element_type=F32)


def centre(values):
    centred = values - jnp.mean(values, -1, keepdims=True)
    return centred, lax.rsqrt(jnp.mean(centred * centred, -1, keepdims=True) + 1e-06)


def norm_back(grad, normed, scale, gain):
    scaled = grad * gain
    return scale * (
        scaled
        - jnp.mean(scaled, -1, keepdims=True)
        - normed * jnp.mean(scaled * normed, -1, keepdims=True)
    )


def gelu_parts(v):
    phi = 0.5 + 0.5 * lax.erf(v * 0.7071067811865476)
    return phi, phi + v * (0.3989422804014327 * jnp.exp(-0.5 * v * v))


def layer(
    sizes,
    patches, cotangent, gain_one, shift_one, token_in, token_bias, token_out, token_shift,
    gain_two, shift_two, channel_in, channel_bias, channel_out, channel_shift,
    mixed, keep, summed, hid_out, slope_out,
    wi, wo, cbo, twi, two, twi_t, two_t,
    dys, dys_t, u2s, u2s_t, u1s, chid, dcp, dtok,
    xs, ms, hid, slope, stats,
    row_acc, cb_acc, ts_acc, tin_acc, tout_acc, small,
    grads, from_core, own, oth, from_mp, from_x, from_z, from_far,
    load_sem, stage_sem, tok_s, tok_r, w_s, w_r, c_s, c_r, y_s, y_r, x_s, x_r, z_s, z_r,
    a_s, a_r, l_sem, xa_s, xa_r, ca_s, ca_r, far_s, far_r,
):
    images, patch, width, token_half, hidden_half, ticks, dp_size = sizes
    rows = dys.shape[0]
    high = u1s.shape[1]
    step = hidden_half // ticks
    chunks = 2 * ticks
    all_chunks = chunks + 1
    eighth_in, eighth_out = width // 8, step // 8
    half, piece = width // 2, width // 8

    dp = lax.axis_index("dp")
    mp = lax.axis_index("mp")
    core = lax.rem(dp, 2)
    side = lax.rem(lax.div(dp, 2), 2)
    near = lax.rem(lax.div(dp, 2), 4)
    line = lax.rem(lax.div(dp, 4), 4)
    part = core * 4 + near

    to_mp = {"mp": 1 - mp}
    to_core = {"dp": dp + 1 - 2 * core}
    to_side = {"dp": dp + 2 - 4 * side}

    def near_of(r):
        return {"dp": dp + 2 * (lax.rem(near + r, 4) - near)}

    def line_of(r):
        return {"dp": dp + 4 * (lax.rem(line + r, 4) - line)}

    far_bits = []
    bit = 16
    while bit < dp_size:
        far_bits.append(bit)
        bit *= 2

    def far_of(i):
        b = far_bits[i]
        return {"dp": dp + b - 2 * b * lax.rem(lax.div(dp, b), 2)}

    def remote(src, dst, send, recv, device):
        return pltpu.make_async_remote_copy(
            src_ref=src, dst_ref=dst, send_sem=send, recv_sem=recv, device_id=device, device_id_type=MESH
        )

    def al(v, m):
        return pl.multiple_of(v, m)

    def own_loads(t):
        return (
            pltpu.make_async_copy(
                channel_in.at[:, pl.ds(al(t * step, step), step)],
                wi.at[:, pl.ds(al(t * 2 * step, step), step)],
                load_sem.at[t, 0],
            ),
            pltpu.make_async_copy(
                channel_out.at[pl.ds(al(t * step, step), step), :],
                wo.at[pl.ds(al(t * 2 * step, step), step), :],
                load_sem.at[t, 1],
            ),
        )

    def other_in(t, first, count):
        return wi.at[pl.ds(al(first, eighth_in), count), pl.ds(al(t * 2 * step + step, step), step)]

    def other_out(t, first, count):
        return wo.at[pl.ds(al(t * 2 * step + step + first, eighth_out), count), :]

    def gather_mp(t):
        return (
            remote(
                channel_in.at[pl.ds(al(part * eighth_in, eighth_in), eighth_in), pl.ds(al(t * step, step), step)],
                other_in(t, part * eighth_in, eighth_in),
                w_s.at[0, t, 0], w_r.at[0, t, 0], to_mp,
            ),
            remote(
                channel_out.at[pl.ds(al(t * step + part * eighth_out, eighth_out), eighth_out), :],
                other_out(t, part * eighth_out, eighth_out),
                w_s.at[0, t, 1], w_r.at[0, t, 1], to_mp,
            ),
        )

    def gather_near(t):
        copies = []
        for r in (1, 2, 3):
            a = other_in(t, part * eighth_in, eighth_in)
            b = other_out(t, part * eighth_out, eighth_out)
            copies.append(remote(a, a, w_s.at[r, t, 0], w_r.at[r, t, 0], near_of(r)))
            copies.append(remote(b, b, w_s.at[r, t, 1], w_r.at[r, t, 1], near_of(r)))
        return copies

    def gather_core(t):
        a = other_in(t, core * 4 * eighth_in, 4 * eighth_in)
        b = other_out(t, core * 4 * eighth_out, 4 * eighth_out)
        return (
            remote(a, a, w_s.at[4, t, 0], w_r.at[4, t, 0], to_core),
            remote(b, b, w_s.at[4, t, 1], w_r.at[4, t, 1], to_core),
        )

    def token_sends():
        return (
            remote(twi.at[pl.ds(0, token_half)], twi.at[pl.ds(token_half, token_half)], tok_s.at[0], tok_r.at[0], to_mp),
            remote(two.at[pl.ds(0, token_half)], two.at[pl.ds(token_half, token_half)], tok_s.at[1], tok_r.at[1], to_mp),
            remote(channel_bias, cbo, tok_s.at[2], tok_r.at[2], to_mp),
        )

    def core_copy(c):
        slot, q = lax.rem(lax.div(c, 2), 2), lax.rem(c, 2)
        return remote(grads.at[slot, 1 - core, q], from_core.at[slot, q], c_s.at[c], c_r.at[c], to_core)

    def mp_copy(c):
        return remote(oth.at[c], from_mp.at[c], y_s.at[c], y_r.at[c], to_mp)

    def side_copy(c):
        return remote(own.at[c, pl.ds(al((1 - side) * half, half), half)], from_x.at[c], x_s.at[c], x_r.at[c], to_side)

    def mine(c):
        return own.at[c, pl.ds(al(side * half + line * piece, piece), piece)]

    def my_sum(c):
        return summed.at[core, c, pl.ds(al(side * half + line * piece, piece), piece)]

    def line_copies(c):
        return [
            remote(
                own.at[c, pl.ds(al(side * half + lax.rem(line + r, 4) * piece, piece), piece)],
                from_z.at[c, r - 1], z_s.at[c, r - 1], z_r.at[c, r - 1], line_of(r),
            )
            for r in (1, 2, 3)
        ]

    def keep_copy(c):
        return pltpu.make_async_copy(mine(c), my_sum(c), l_sem.at[c])

    def spread_copies(c):
        return [
            remote(mine(c), my_sum(c), a_s.at[c, r - 1], a_r.at[c, r - 1], line_of(r)) for r in (1, 2, 3)
        ]

    def side_spread(c):
        ref = summed.at[core, c, pl.ds(al(side * half, half), half)]
        return remote(ref, ref, xa_s.at[c], xa_r.at[c], to_side)

    def core_spread(c):
        ref = summed.at[core, c]
        return remote(ref, ref, ca_s.at[c], ca_r.at[c], to_core)

    def add(a, b):
        return (a.astype(F32) + b.astype(F32)).astype(BF16)

    def after_core(c):
        core_copy(c).wait()
        slot, q = lax.rem(lax.div(c, 2), 2), lax.rem(c, 2)
        oth[c] = add(grads[slot, core, q, 1], from_core[slot, q, 1])
        mp_copy(c).start()
        own[c] = add(grads[slot, core, q, 0], from_core[slot, q, 0])

    def after_mp(c):
        mp_copy(c).wait()
        own[c] = add(own[c], from_mp[c])
        side_copy(c).start()

    def after_side(c):
        side_copy(c).wait()
        rng = pl.ds(al(side * half, half), half)
        own[c, rng] = add(own[c, rng], from_x[c])
        for copy in line_copies(c):
            copy.start()

    def after_line(c):
        for copy in line_copies(c):
            copy.wait()
        rng = pl.ds(al(side * half + line * piece, piece), piece)
        total = own[c, rng].astype(F32)
        for r in range(3):
            total = total + from_z[c, r].astype(F32)
        own[c, rng] = total.astype(BF16)
        for i in range(len(far_bits)):
            copy = remote(mine(c), from_far.at[c, i], far_s.at[c, i], far_r.at[c, i], far_of(i))
            copy.start()
            copy.wait()
            own[c, rng] = add(own[c, rng], from_far[c, i])
        keep_copy(c).start()
        for copy in spread_copies(c):
            copy.start()

    def after_spread(c):
        keep_copy(c).wait()
        for copy in spread_copies(c):
            copy.wait()
        side_spread(c).start()

    def after_side_spread(c):
        side_spread(c).wait()
        core_spread(c).start()

    def after_core_spread(c):
        core_spread(c).wait()

    stages = (after_mp, after_side, after_line, after_spread, after_side_spread, after_core_spread)

    def point(p, with_core):
        if with_core:
            c = p - 2

            @pl.when(jnp.logical_and(c >= 0, c < chunks))
            def _():
                after_core(c)

        for offset, stage in zip(OFFSETS, stages):
            k = p - offset
            c = lax.div(DEN * k + DEN - 1, NUM)
            hit = jnp.logical_and(lax.div(NUM * c, DEN) == k, jnp.logical_and(k >= 0, c < all_chunks))

            @pl.when(hit)
            def _(c=c, stage=stage):
                stage(c)

    barrier = pltpu.get_barrier_semaphore()
    greet = [to_mp, to_core] + [near_of(r) for r in (1, 2, 3)] + [line_of(r) for r in (1, 2, 3)]
    greet += [far_of(i) for i in range(len(far_bits))]
    for device in greet:
        pl.semaphore_signal(barrier, inc=1, device_id=device, device_id_type=MESH)

    def patch_copy(b):
        return pltpu.make_async_copy(patches.at[b], xs.at[lax.rem(b, 2)], stage_sem.at[0, lax.rem(b, 2)])

    def cot_copy(b):
        return pltpu.make_async_copy(cotangent.at[b], ms.at[lax.rem(b, 2)], stage_sem.at[1, lax.rem(b, 2)])

    def hid_save(b):
        s = lax.rem(b, 2)
        return (
            pltpu.make_async_copy(hid.at[s], hid_out.at[b], stage_sem.at[2, s]),
            pltpu.make_async_copy(slope.at[s], slope_out.at[b], stage_sem.at[3, s]),
        )

    def hid_load(b):
        s = lax.rem(b, 2)
        return (
            pltpu.make_async_copy(hid_out.at[b], hid.at[s], stage_sem.at[2, s]),
            pltpu.make_async_copy(slope_out.at[b], slope.at[s], stage_sem.at[3, s]),
        )

    def mixed_save(b):
        s = lax.rem(b, 2)
        return pltpu.make_async_copy(ms.at[s], mixed.at[b], stage_sem.at[4, s])

    def both(copies, what):
        for copy in copies:
            getattr(copy, what)()

    for b in (0, 1):
        cot_copy(b).start()
        patch_copy(b).start()

    def start_own(t, _):
        both(own_loads(t), "start")
        return 0

    lax.fori_loop(0, ticks, start_own, 0)

    wide = twi.shape[1]
    bias = token_bias[...]
    bias_hi = bias.astype(BF16)
    rest = bias - bias_hi.astype(F32)
    bias_mid = rest.astype(BF16)
    bias_lo = (rest - bias_mid.astype(F32)).astype(BF16)
    zero_half = jnp.zeros((token_half, wide), BF16)
    twi[pl.ds(0, token_half), :] = zero_half
    two[pl.ds(0, token_half), :] = zero_half
    twi[pl.ds(0, token_half), pl.ds(0, patch)] = token_in[...].T
    two[pl.ds(0, token_half), pl.ds(0, patch)] = token_out[...]
    lane = lax.broadcasted_iota(jnp.int32, (token_half, wide), 1)
    filled = twi[pl.ds(0, token_half), :].astype(F32)
    filled = jnp.where(lane == patch, bias_hi.astype(F32), filled)
    filled = jnp.where(lane == patch + 1, bias_mid.astype(F32), filled)
    filled = jnp.where(lane == patch + 2, bias_lo.astype(F32), filled)
    twi[pl.ds(0, token_half), :] = filled.astype(BF16)

    pl.semaphore_wait(barrier, len(greet))
    both(token_sends(), "start")

    def start_mp(t, _):
        both(gather_mp(t), "start")
        return 0

    lax.fori_loop(0, ticks, start_mp, 0)

    dys[...] = jnp.zeros_like(dys)
    u2s[...] = jnp.zeros_like(u2s)
    dtok[...] = jnp.zeros_like(dtok)
    rest_rows = rows - images * high
    if rest_rows:
        chid[pl.ds(images * high, rest_rows), :] = jnp.zeros((rest_rows, chid.shape[1]), BF16)
        dcp[pl.ds(images * high, rest_rows), :] = jnp.zeros((rest_rows, dcp.shape[1]), BF16)
    row_acc[...] = jnp.zeros_like(row_acc)
    ts_acc[...] = jnp.zeros_like(ts_acc)
    tin_acc[...] = jnp.zeros_like(tin_acc)
    tout_acc[...] = jnp.zeros_like(tout_acc)
    small[...] = jnp.zeros_like(small)
    u2s_t[pl.ds(width, 16), :] = jnp.ones((16, rows), BF16)

    below = lax.broadcasted_iota(jnp.int32, (high, width), 0)
    ones = jnp.where(jnp.logical_and(below >= patch, below < patch + 3), 1.0, 0.0).astype(BF16)
    for b in range(images):
        u1s[b] = ones

    def take_cot(b, _):
        s = lax.rem(b, 2)
        cot_copy(b).wait()
        value = ms[s]
        dys[pl.ds(al(b * high, 16), patch), :] = value
        row_acc[pl.ds(4, 1), :] += jnp.sum(value.astype(F32), 0, keepdims=True)

        @pl.when(b + 2 < images)
        def _():
            cot_copy(b + 2).start()

        return 0

    lax.fori_loop(0, images, take_cot, 0)

    def turn_dy(j, _):
        at = pl.ds(al(j * LANES, LANES), LANES)
        dys_t[:, at] = dys[at, :].T
        return 0

    lax.fori_loop(0, rows // LANES, turn_dy, 0)

    both(token_sends(), "wait")
    twi_t[...] = twi[...].T
    two_t[...] = two[...].T

    def token_forward(b, _):
        s = lax.rem(b, 2)
        patch_copy(b).wait()
        x = xs[s].astype(F32)

        @pl.when(b + 2 < images)
        def _():
            patch_copy(b + 2).start()

        mean = jnp.mean(x, -1, keepdims=True)
        centred = x - mean
        scale = lax.rsqrt(jnp.mean(centred * centred, -1, keepdims=True) + 1e-06)
        stats[b, :, 0:1] = mean
        stats[b, :, 1:2] = scale
        u1s[b, pl.ds(0, patch), :] = (centred * scale * gain_one[...] + shift_one[...]).astype(BF16)
        pre = dot(twi[:, pl.ds(0, high)], u1s[b])
        phi, deriv = gelu_parts(pre)

        @pl.when(b >= 2)
        def _():
            both(hid_save(b - 2), "wait")

        hidden = (pre * phi).astype(BF16)
        hid[s] = hidden
        slope[s] = deriv.astype(BF16)
        both(hid_save(b), "start")
        tok = dot(two_t[pl.ds(0, high), :], hidden)
        x1 = x + tok[:patch] + token_shift[...]
        keep[b] = x1
        mean = jnp.mean(x1, -1, keepdims=True)
        centred = x1 - mean
        scale = lax.rsqrt(jnp.mean(centred * centred, -1, keepdims=True) + 1e-06)
        stats[b, :, 2:3] = mean
        stats[b, :, 3:4] = scale
        u2s[pl.ds(al(b * high, 16), patch), :] = (centred * scale * gain_two[...] + shift_two[...]).astype(BF16)

        @pl.when(b < ticks)
        def _():
            both(gather_mp(b), "wait")
            both(gather_near(b), "start")

        return 0

    lax.fori_loop(0, images, token_forward, 0)
    for t in range(images, ticks):
        both(gather_mp(t), "wait")
        both(gather_near(t), "start")
    both(gather_near(0), "wait")
    both(gather_core(0), "start")

    def turn_u2(j, _):
        at = pl.ds(al(j * LANES, LANES), LANES)
        u2s_t[pl.ds(0, width), at] = u2s[at, :].T
        return 0

    lax.fori_loop(0, rows // LANES, turn_u2, 0)
    for b in range(max(images - 2, 0), images):
        both(hid_save(b), "wait")

    live = images * high
    tiles = 2 if live % 32 == 0 else 1
    tall = live // tiles

    def channel(t, _):
        both(own_loads(t), "wait")
        both(gather_core(t), "wait")
        at = pl.ds(al(t * 2 * step, 2 * step), 2 * step)
        weight_in, weight_out = wi[:, at], wo[at, :]
        here = pl.ds(al(t * step, step), step)
        bias = jnp.concatenate([channel_bias[:, here], cbo[:, here]], axis=1)
        for i in range(tiles):
            rng = pl.ds(i * tall, tall)
            pre = dot(u2s[rng, :], weight_in) + bias
            back = dot_nt(dys[rng, :], weight_out)
            phi, deriv = gelu_parts(pre)
            chid[rng, at] = (pre * phi).astype(BF16)
            dcp[rng, at] = (back * deriv).astype(BF16)

        @pl.when(t + 1 < ticks)
        def _():
            both(gather_near(t + 1), "wait")
            both(gather_core(t + 1), "start")

        point(2 * t, True)
        slot = lax.rem(t, 2)
        grad_in = dot(u2s_t[...], dcp[:, at])
        cb_acc[:, at] = grad_in[width : width + 1]
        grad_in = grad_in[:width].astype(BF16)
        grad_out = dot(dys_t[...], chid[:, at]).astype(BF16)
        for m, value in ((0, grad_in), (1, grad_out)):
            for o in (0, 1):
                for q in (0, 1):
                    first = o * step + q * LANES
                    grads[slot, m, q, o] = value[:, first : first + LANES]
        point(2 * t + 1, True)
        core_copy(2 * t).start()
        core_copy(2 * t + 1).start()
        return 0

    lax.fori_loop(0, ticks, channel, 0)

    both(hid_load(0), "start")
    patch_copy(0).start()
    ones16 = jnp.ones((16, width), BF16)

    def backward(b, _):
        s = lax.rem(b, 2)
        rng = pl.ds(al(b * high, 16), high)

        @pl.when(b + 1 < images)
        def _():
            both(hid_load(b + 1), "start")
            patch_copy(b + 1).start()

        @pl.when(b >= 2)
        def _():
            mixed_save(b - 2).wait()

        x1 = keep[b]
        ms[s] = (x1 + dot(chid[rng, :], wo[...])[:patch] + channel_shift[...]).astype(BF16)
        mixed_save(b).start()
        du2 = dot_nt(dcp[rng, :], wi[...])[:patch]
        n2 = (x1 - stats[b, :, 2:3]) * stats[b, :, 3:4]
        row_acc[pl.ds(2, 1), :] += jnp.sum(du2 * n2, 0, keepdims=True)
        row_acc[pl.ds(3, 1), :] += jnp.sum(du2, 0, keepdims=True)
        dy = dys[pl.ds(al(b * high, 16), patch), :].astype(F32)
        dx1 = dy + norm_back(du2, n2, stats[b, :, 3:4], gain_two[...])
        keep[b] = dx1
        dtok[pl.ds(0, patch), :] = dx1.astype(BF16)
        point(chunks + 2 * b, True)
        both(hid_load(b), "wait")
        dtk = dtok[...]
        hidden = hid[s]
        tout_acc[:, pl.ds(0, high)] += dot_nt(hidden, dtk)
        ts_acc[:, pl.ds(0, high)] += dot_nt(ones16, dtk)
        dpre = (dot(two[:, pl.ds(0, high)], dtk) * slope[s].astype(F32)).astype(BF16)
        tin_acc[:, pl.ds(0, high)] += dot_nt(dpre, u1s[b])
        du1 = dot(twi_t[pl.ds(0, high), :], dpre)[:patch]
        patch_copy(b).wait()
        n1 = (xs[s].astype(F32) - stats[b, :, 0:1]) * stats[b, :, 1:2]
        row_acc[pl.ds(0, 1), :] += jnp.sum(du1 * n1, 0, keepdims=True)
        row_acc[pl.ds(1, 1), :] += jnp.sum(du1, 0, keepdims=True)
        keep[b] = keep[b] + norm_back(du1, n1, stats[b, :, 1:2], gain_one[...])
        point(chunks + 2 * b + 1, True)
        return 0

    lax.fori_loop(0, images, backward, 0)

    blocks = width // LANES
    for o in (0, 1):
        for v in range(5):
            for j in range(blocks):
                small[o, pl.ds(v * blocks + j, 1), :] = row_acc[pl.ds(v, 1), pl.ds(j * LANES, LANES)]
        for j in range(2):
            small[o, pl.ds(5 * blocks + j, 1), :] = ts_acc[pl.ds(0, 1), pl.ds(j * LANES, LANES)]
        for c in range(chunks):
            first = (c // 2) * 2 * step + o * step + (c % 2) * LANES
            small[o, pl.ds(5 * blocks + 2 + c, 1), :] = cb_acc[pl.ds(0, 1), pl.ds(first, LANES)]
    last_slot = ticks % 2
    for o in (0, 1):
        for m, acc in ((0, tin_acc), (1, tout_acc)):
            for j in range(2):
                grads[last_slot, m, 0, o, pl.ds(j * token_half, token_half), :] = acc[
                    pl.ds(o * token_half, token_half), pl.ds(j * LANES, LANES)
                ].astype(BF16)
        grads[last_slot, 0, 0, o, pl.ds(2 * token_half, small.shape[1]), :] = small[o].astype(BF16)
    core_copy(chunks).start()
    after_core(chunks)

    def drain(p, _):
        point(p, False)
        return 0

    first = chunks + 2 * images
    lax.fori_loop(first, OFFSETS[-1] + (NUM * chunks) // DEN + 1, drain, 0)
    for b in range(max(images - 2, 0), images):
        mixed_save(b).wait()


def widen(sizes, chunk, last, d_in, d_out, d_tin, d_tbias, d_tout, d_tshift, d_rows, d_cbias):
    patch, width, token_half, chunks = sizes
    d_in[...] = chunk[0, 0].astype(F32)
    d_out[...] = chunk[1, 0].astype(F32).T

    @pl.when(pl.program_id(0) == 0)
    def _():
        both = [
            jnp.concatenate(
                [last[m, 0, pl.ds(0, token_half), :], last[m, 0, pl.ds(token_half, token_half), :]], axis=1
            ).astype(F32)
            for m in (0, 1)
        ]
        turned = both[0].T
        d_tin[...] = turned[:patch]
        d_tbias[...] = turned[patch : patch + 1]
        d_tout[...] = both[1][:, :patch]
        blocks = width // LANES
        rows = last[0, 0, pl.ds(2 * token_half, 64), :].astype(F32)
        for v in range(5):
            for j in range(blocks):
                i = v * blocks + j
                d_rows[pl.ds(v, 1), pl.ds(j * LANES, LANES)] = rows[i : i + 1]
        i = 5 * blocks
        d_tshift[...] = jnp.concatenate([rows[i : i + 1], rows[i + 1 : i + 2]], axis=1)[:, :patch]
        for c in range(chunks):
            i = 5 * blocks + 2 + c
            d_cbias[pl.ds(0, 1), pl.ds(c * LANES, LANES)] = rows[i : i + 1]


def per_device(
    dp_size,
    patches, cotangent, gain_one, shift_one, token_in, token_bias, token_out, token_shift,
    gain_two, shift_two, channel_in, channel_bias, channel_out, channel_shift,
):
    images, patch, width = patches.shape
    token_half = token_in.shape[1]
    hidden_half = channel_in.shape[1]
    step = 2 * LANES
    ticks = hidden_half // step
    chunks = 2 * ticks
    high = -(-(patch + 3) // 16) * 16
    rows = -(-images * high // LANES) * LANES
    wide = -(-patch // LANES) * LANES
    tokens = 2 * token_half
    far = max(sum(1 for b in range(4, 20) if 2**b < dp_size), 1)
    far_chunks = chunks + 1 if dp_size > 16 else 1
    sizes = (images, patch, width, token_half, hidden_half, ticks, dp_size)
    vmem = pl.BlockSpec(memory_space=pltpu.VMEM)
    hbm = pl.BlockSpec(memory_space=pl.ANY)
    n = chunks + 1
    dma = pltpu.SemaphoreType.DMA
    mixed, inputs_grad, summed, _, _ = pl.pallas_call(
        functools.partial(layer, sizes),
        out_shape=(
            jax.ShapeDtypeStruct((images, patch, width), BF16),
            jax.ShapeDtypeStruct((images, patch, width), F32),
            jax.ShapeDtypeStruct((2, n, width, LANES), BF16),
            jax.ShapeDtypeStruct((images, tokens, width), BF16),
            jax.ShapeDtypeStruct((images, tokens, width), BF16),
        ),
        in_specs=[hbm, hbm, vmem, vmem, vmem, vmem, vmem, vmem, vmem, vmem, hbm, vmem, hbm, vmem],
        out_specs=(hbm, vmem, hbm, hbm, hbm),
        scratch_shapes=[
            pltpu.VMEM((width, 2 * hidden_half), BF16),
            pltpu.VMEM((2 * hidden_half, width), BF16),
            pltpu.VMEM((1, hidden_half), F32),
            pltpu.VMEM((tokens, wide), BF16),
            pltpu.VMEM((tokens, wide), BF16),
            pltpu.VMEM((wide, tokens), BF16),
            pltpu.VMEM((wide, tokens), BF16),
            pltpu.VMEM((rows, width), BF16),
            pltpu.VMEM((width, rows), BF16),
            pltpu.VMEM((rows, width), BF16),
            pltpu.VMEM((width + 16, rows), BF16),
            pltpu.VMEM((images, high, width), BF16),
            pltpu.VMEM((rows, 2 * hidden_half), BF16),
            pltpu.VMEM((rows, 2 * hidden_half), BF16),
            pltpu.VMEM((high, width), BF16),
            pltpu.VMEM((2, patch, width), BF16),
            pltpu.VMEM((2, patch, width), BF16),
            pltpu.VMEM((2, tokens, width), BF16),
            pltpu.VMEM((2, tokens, width), BF16),
            pltpu.VMEM((images, patch, 4), F32),
            pltpu.VMEM((8, width), F32),
            pltpu.VMEM((1, 2 * hidden_half), F32),
            pltpu.VMEM((16, wide), F32),
            pltpu.VMEM((tokens, wide), F32),
            pltpu.VMEM((tokens, wide), F32),
            pltpu.VMEM((2, 64, LANES), F32),
            pltpu.VMEM((2, 2, 2, 2, width, LANES), BF16),
            pltpu.VMEM((2, 2, 2, width, LANES), BF16),
            pltpu.VMEM((n, width, LANES), BF16),
            pltpu.VMEM((n, width, LANES), BF16),
            pltpu.VMEM((n, width, LANES), BF16),
            pltpu.VMEM((n, width // 2, LANES), BF16),
            pltpu.VMEM((n, 3, width // 8, LANES), BF16),
            pltpu.VMEM((far_chunks, far, width // 8, LANES), BF16),
            dma((ticks, 2)),
            dma((5, 2)),
            dma((3,)), dma((3,)),
            dma((5, ticks, 2)), dma((5, ticks, 2)),
            dma((n,)), dma((n,)),
            dma((n,)), dma((n,)),
            dma((n,)), dma((n,)),
            dma((n, 3)), dma((n, 3)),
            dma((n, 3)), dma((n, 3)),
            dma((n,)),
            dma((n,)), dma((n,)),
            dma((n,)), dma((n,)),
            dma((far_chunks, far)), dma((far_chunks, far)),
        ],
        compiler_params=pltpu.CompilerParams(
            collective_id=0, has_side_effects=True, vmem_limit_bytes=63 * 2**20
        ),
        name="mixer_layer",
    )(
        patches, cotangent, gain_one.reshape(1, -1), shift_one.reshape(1, -1), token_in,
        token_bias.reshape(-1, 1), token_out, token_shift.reshape(-1, 1), gain_two.reshape(1, -1),
        shift_two.reshape(1, -1), channel_in, channel_bias.reshape(1, -1), channel_out,
        channel_shift.reshape(1, -1),
    )

    def whole(*shape):
        return pl.BlockSpec(shape, lambda c: (0,) * len(shape))

    d_in, d_out, d_tin, d_tbias, d_tout, d_tshift, d_rows, d_cbias = pl.pallas_call(
        functools.partial(widen, (patch, width, token_half, chunks)),
        grid=(chunks,),
        in_specs=[
            pl.BlockSpec((2, 1, width, LANES), lambda c: (0, c, 0, 0)),
            pl.BlockSpec((2, 1, width, LANES), lambda c: (0, chunks, 0, 0)),
        ],
        out_specs=(
            pl.BlockSpec((width, LANES), lambda c: (0, c)),
            pl.BlockSpec((LANES, width), lambda c: (c, 0)),
            whole(patch, token_half), whole(1, token_half), whole(token_half, patch), whole(1, patch),
            whole(8, width), whole(1, hidden_half),
        ),
        out_shape=(
            jax.ShapeDtypeStruct((width, hidden_half), F32),
            jax.ShapeDtypeStruct((hidden_half, width), F32),
            jax.ShapeDtypeStruct((patch, token_half), F32),
            jax.ShapeDtypeStruct((1, token_half), F32),
            jax.ShapeDtypeStruct((token_half, patch), F32),
            jax.ShapeDtypeStruct((1, patch), F32),
            jax.ShapeDtypeStruct((8, width), F32),
            jax.ShapeDtypeStruct((1, hidden_half), F32),
        ),
        compiler_params=pltpu.CompilerParams(vmem_limit_bytes=32 * 2**20),
        name="widen",
    )(summed, summed)
    return (
        mixed, inputs_grad, d_rows[0], d_rows[1], d_tin, d_tbias[0], d_tout, d_tshift[0],
        d_rows[2], d_rows[3], d_in, d_cbias[0], d_out, d_rows[4],
    )


def solution(mesh):
    split = P(("dp", "mp"), None, None)
    columns, rows, vector = P(None, "mp"), P("mp", None), P("mp")
    return jax.shard_map(
        functools.partial(per_device, mesh.shape["dp"]),
        mesh=mesh,
        in_specs=(
            split, split, P(), P(), columns, vector, rows, P(), P(), P(), columns, vector, rows, P(),
        ),
        out_specs=(
            split, split, P(), P(), columns, vector, rows, P(), P(), P(), columns, vector, rows, P(),
        ),
        check_vma=False,
    )
```

time: 780 us -> 157 us (0.20)
  waiting for transfers between devices: 425 us -> 0 us
  matrix products: 179 us -> 0 us
  Pallas kernels: 0 us -> 135 us
  blocking collectives: 73.9 us -> 0 us
  other arithmetic: 37.8 us -> 0.62 us
  local copies, waits for them, and re-layouts: 40.4 us -> 20.6 us
  between operations: 14.6 us -> 0.67 us
    all_gather x4 -> x0, waiting for transfers between devices: 196 us -> none  [the longest x1 53.8 us: per_device(): gathered_one = lax.all_gather(mixer_rows, 'mp', axis=0, tiled=True)]
    dot_general x12 -> x0, matrix products: 179 us -> none  [the longest x1 44.2 us: per_device(): jnp.dot(channel_hidden, mat_out, preferred_element_type=jnp.float32)]
    pallas_call x0 -> x2, Pallas kernels: none -> 135 us  [the longest x1 128 us: per_device(): pl.pallas_call(functools.partial(layer, sizes), out_shape=(jax.ShapeDtype...]
    psum x1 -> x0, waiting for transfers between devices: 131 us -> none  [per_device(): lax.psum((tokenin_grad, tokenbias_grad, tokenout_grad, channelin_grad, ch...]
    reduce_scatter x4 -> x0, waiting for transfers between devices: 97.6 us -> none  [the longest x1 48.9 us: per_device(): lax.psum_scatter(second_part.astype(jnp.bfloat16), 'mp', scatter_dimensio...]
    psum x2 -> x0, blocking collectives: 73.9 us -> none  [the longest x1 39.1 us: per_device(): lax.psum((gainone_grad, shiftone_grad, tokenshift_grad, gaintwo_grad, shi...]
    reduce_sum x7 -> x0, other arithmetic: 23.7 us -> none  [the longest x1 5.78 us: per_device(): tokenshift_grad = jnp.sum(branch_grad.astype(jnp.float32), (0, 2))]
    convert_element_type x2 -> x0, local copies, waits for them, and re-layouts: 11.5 us -> none  [the longest x1 5.75 us: per_device(): second_part.astype(jnp.bfloat16)]
  transfers between devices with their start and end apart: 9 -> 0, of which waited for: 7 -> 0; matrix products, arithmetic and copies ran while one was open for 14% -> 0% of each run, Pallas kernels for 0% -> 0%
where the time goes in v1:
time: 157 us
  Pallas kernels  135 us (86%)
  local copies, waits for them, and re-layouts  20.6 us (13%)
    pallas_call x1, Pallas kernels, per_device(): pl.pallas_call(functools.partial(layer, sizes), out_shape=(jax.ShapeDtype...  128 us
    unnamed x10, local copies, waits for them, and re-layouts  9.43 us
    pallas_call x1, Pallas kernels, per_device(): pl.pallas_call(functools.partial(widen, (patch, width, token_half, chunks...  6.73 us

profile of v1, /device:TPU:0, one launch (start us, length us, event | category | flops | bytes accessed | tf_op | source)
XLA Modules:
  0.0 156.8 jit_solution(9891020468348451783)
XLA Ops:
  0.6 1.3 reshape.52.gain_one
  1.9 1.3 reshape.53.shift_one
  3.2 1.3 reshape.56.gain_two
  4.4 1.3 reshape.57.shift_two
  5.7 1.3 reshape.59.channel_shift
  7.0 1.3 reshape.58.channel_bias
  8.3 1.4 copy.31.token_bias
  9.7 1.6 %copy.30.token_in = bf16[196,192]{1,0:T(8,128)(2,1)} copy(bf16[196,192]{0,1:T(8,128)(2,1)} %param.18) | data formatting | bytes 150528 | tf_op args[4]
  11.4 1.4 copy.32.token_shift
  12.8 128.2 %mixer_layer.1 = (bf16[6,196,768]{2,1,0:T(8,128)(2,1)}, f32[6,196,768]{2,1,0:T(8,128)}, bf16[2,13,768,128]{3,2,1,0:T(8,128)(2,1)}, bf16[6,384,768]{2,1,0:T(8,128)(2,1)}, bf16[6,384,768]{2,1,0:T(8,128)(2,1)}) custom-call(bf16[6,196,768]{2,1,0:T(8,128)(2,1)} %patches.1, bf16[6,196,768]{2,1,0:T(8,128)(2,1)} %cotangent.1, f32[1,768]{1,0:T(1,128)} %reshape.52.gain_one, ...), custom_call_target="tpu_custom_call" | custom-call | tf_op jit(solution)/shard_map/mixer_layer/pallas_call | solution.py:621
  141.0 0.0 copy-start
  141.0 2.4 %copy-done = bf16[2,13,768,128]{3,2,1,0:T(8,128)(2,1)S(1)} copy-done((bf16[2,13,768,128]{3,2,1,0:T(8,128)(2,1)S(1)}, bf16[2,13,768,128]{3,2,1,0:T(8,128)(2,1)}, u32[]{:S(2)}) %copy-start) | copy-done | bytes 5111832
  143.4 0.0 copy-start.2
  143.4 6.7 %widen.1 = (f32[768,1536]{1,0:T(8,128)}, f32[1536,768]{1,0:T(8,128)}, f32[196,192]{1,0:T(8,128)S(1)}, f32[1,192]{1,0:T(1,128)}, f32[192,196]{1,0:T(8,128)}, /*in...) custom-call(bf16[2,13,768,128]{3,2,1,0:T(8,128)(2,1)S(1)} %copy-done, bf16[2,13,768,128]{3,2,1,0:T(8,128)(2,1)S(1)} %copy-done), custom_call_target="tpu_custom_call" | custom-call | tf_op jit(solution)/shard_map/widen/pallas_call | solution.py:695
  150.2 0.6 slice_reduce_fusion
  150.8 0.6 reduce.4
  151.4 0.8 copy.33
  152.2 0.0 copy-done.2
  152.2 0.0 copy-start.1
  152.2 1.2 copy.36
  153.4 1.5 copy-done.1
  154.9 1.8 %copy.37 = f32[6,196,768]{2,1,0:T(8,128)} copy(f32[6,196,768]{2,1,0:T(8,128)S(1)} %copy-done.1) | data formatting | bytes 7225344
Async XLA Ops:
  141.0 2.5 %copy-start = (bf16[2,13,768,128]{3,2,1,0:T(8,128)(2,1)S(1)}, bf16[2,13,768,128]{3,2,1,0:T(8,128)(2,1)}, u32[]{:S(2)}) copy-start(bf16[2,13,768,128]{3,2,1,0:T(8,128)(2,1)} %get-tuple-element.27.chunk.last) | copy-start | bytes 15335428
  143.4 8.8 %copy-start.2 = (bf16[6,196,768]{2,1,0:T(8,128)(2,1)S(1)}, bf16[6,196,768]{2,1,0:T(8,128)(2,1)}, u32[]{:S(2)}) copy-start(bf16[6,196,768]{2,1,0:T(8,128)(2,1)} %get-tuple-element.83) | copy-start | bytes 5419012
  152.2 2.7 %copy-start.1 = (f32[6,196,768]{2,1,0:T(8,128)S(1)}, f32[6,196,768]{2,1,0:T(8,128)}, u32[]{:S(2)}) copy-start(f32[6,196,768]{2,1,0:T(8,128)} %get-tuple-element.84) | copy-start | bytes 10838020

commit v2 on v1

v2 whole, which is shorter than its diff:
```python
import functools

import jax
import jax.numpy as jnp
from jax import lax
from jax.experimental import pallas as pl
from jax.experimental.pallas import tpu as pltpu
from jax.sharding import PartitionSpec as P

MESH = pl.DeviceIdType.MESH
F32 = jnp.float32
BF16 = jnp.bfloat16
NT = (((1,), (1,)), ((), ()))
LANES = 128
RING = 4

STRAIGHT = (0, 2, 3, 5, 6, 10, 12)
POINTS = (
    ("core_mp", ((0, 2), (2, 4), (3, 5), (5, 7), (6, 8), (7, 9), (8, 10), (9, 11), (10, 12))),
    ("core_both", ((1, 3), (4, 6), (11, 13))),
    ("mp", ((0, 6), (2, 8), (3, 10), (5, 12), (6, 14), (7, 16), (8, 18), (9, 20), (10, 22))),
    ("both", ((1, 7), (4, 10), (11, 16))),
    ("side", ((7, 18), (8, 20), (9, 23))),
    ("side_line", ((0, 11), (2, 12), (3, 13), (5, 14), (6, 17))),
    ("then_mp", ((1, 12), (4, 18), (11, 23))),
    ("low", ((1, 14), (7, 20), (4, 21), (8, 22))),
    ("high", ((1, 18), (7, 22), (4, 23))),
    ("line", ((0, 13), (2, 14), (3, 15), (5, 17), (6, 20))),
    ("high_spread", ((1, 22),)),
    ("spread", ((0, 16), (2, 18), (3, 20), (5, 21), (6, 23))),
    ("side_spread", ((0, 19), (2, 21), (3, 22))),
    ("core_spread", ((0, 20), (2, 22), (3, 23))),
)
REST = (
    ("low_spread", 1), ("side_spread", 5), ("high_spread", 7), ("core_mp", 12), ("high", 8), ("core_spread", 5),
    ("low", 11), ("side_line", 10), ("low", 9), ("high_spread", 4), ("side_spread", 6), ("low_spread", 7),
    ("high_spread", 8), ("mp", 12), ("core_spread", 6), ("high", 11), ("side_spread", 1), ("line", 10),
    ("core_spread", 1), ("side_spread", 7), ("low_spread", 4), ("high", 9), ("low_spread", 8), ("core_spread", 7),
    ("side_line", 12), ("high_spread", 11), ("spread", 10), ("side_spread", 4), ("high_spread", 9),
    ("core_spread", 4), ("low_spread", 11), ("line", 12), ("side_spread", 8), ("low_spread", 9), ("core_spread", 8),
    ("side_spread", 10), ("spread", 12), ("core_spread", 10), ("side_spread", 11), ("core_spread", 11),
    ("side_spread", 9), ("core_spread", 9), ("side_spread", 12), ("core_spread", 12),
)


def dot(a, b):
    return jnp.dot(a, b, preferred_element_type=F32)


def dot_nt(a, b):
    return lax.dot_general(a, b, NT, preferred_element_type=F32)


def centre(values):
    centred = values - jnp.mean(values, -1, keepdims=True)
    return centred, lax.rsqrt(jnp.mean(centred * centred, -1, keepdims=True) + 1e-06)


def norm_back(grad, normed, scale, gain):
    scaled = grad * gain
    return scale * (
        scaled
        - jnp.mean(scaled, -1, keepdims=True)
        - normed * jnp.mean(scaled * normed, -1, keepdims=True)
    )


def gelu_parts(v):
    phi = 0.5 + 0.5 * lax.erf(v * 0.7071067811865476)
    return phi, phi + v * (0.3989422804014327 * jnp.exp(-0.5 * v * v))


def layer(
    sizes,
    patches, cotangent, gain_one, shift_one, token_in, token_bias, token_out, token_shift,
    gain_two, shift_two, channel_in, channel_bias, channel_out, channel_shift,
    mixed, inputs_grad, summed, hid_out, slope_out,
    wi, wo, vecs, cbs, cbo, tbs, tss, tins, touts, tw, twi_t, two_t, keep,
    dys, dys_t, u2s, u2s_t, u1s, chid, dcp, dtok,
    xs, ms, hid, slope, stats,
    row_acc, cb_acc, tin_acc, tout_acc, small,
    grads, from_core, acc, from_mp, from_x, from_z, from_far,
    load_sem, stage_sem, small_sem, grad_sem, tok_s, tok_r, w_s, w_r, wc_s, wc_r, c_s, c_r, y_s, y_r, x_s, x_r, z_s, z_r, zh_s, zh_r, zl_s, zl_r,
    a_s, a_r, al_s, al_r, sl_s, sl_r, l_sem, xa_s, xa_r, ca_s, ca_r, far_s, far_r,
):
    images, patch, width, token_half, hidden_half, ticks, dp_size, last_half = sizes
    rows = dys.shape[0]
    high = u1s.shape[1]
    step = hidden_half // ticks
    half = width // 2
    chunks = 2 * ticks
    eighth_in = width // 8

    dp = lax.axis_index("dp")
    mp = lax.axis_index("mp")
    core = lax.rem(dp, 2)
    side = lax.rem(lax.div(dp, 2), 2)
    near = lax.rem(lax.div(dp, 2), 4)
    line = lax.rem(lax.div(dp, 4), 4)
    part = core * 4 + near
    low = lax.rem(line, 2)

    to_mp = {"mp": 1 - mp}
    to_core = {"dp": dp + 1 - 2 * core}
    to_side = {"dp": dp + 2 - 4 * side}

    def near_of(r):
        return {"dp": dp + 2 * (lax.rem(near + r, 4) - near)}

    def line_of(r):
        return {"dp": dp + 4 * (lax.rem(line + r, 4) - line)}

    far_bits = []
    bit = 16
    while bit < dp_size:
        far_bits.append(bit)
        bit *= 2

    def far_of(i):
        b = far_bits[i]
        return {"dp": dp + b - 2 * b * lax.rem(lax.div(dp, b), 2)}

    def remote(src, dst, send, recv, device):
        return pltpu.make_async_remote_copy(
            src_ref=src, dst_ref=dst, send_sem=send, recv_sem=recv, device_id=device, device_id_type=MESH
        )

    def al(v, m):
        return pl.multiple_of(v, m)

    def own_loads(t):
        return (
            pltpu.make_async_copy(
                channel_in.at[:, pl.ds(al(t * step, step), step)],
                wi.at[:, pl.ds(al(t * 2 * step, step), step)],
                load_sem.at[t, 0],
            ),
            pltpu.make_async_copy(
                channel_out.at[pl.ds(al(t * step, step), step), :],
                wo.at[pl.ds(al(t * 2 * step, step), step), :],
                load_sem.at[t, 1],
            ),
        )

    def other_in(t, first, count):
        return wi.at[pl.ds(al(first, eighth_in), count), pl.ds(al(t * 2 * step + step, step), step)]

    def other_out(t, first, count):
        return wo.at[pl.ds(al(t * 2 * step + step + first, 16), count), :]

    which = side + core * (low - side)
    quarter_out = step // 4
    to_pair = {"dp": dp + (2 - 4 * side) * (1 - core) + (4 - 8 * low) * core}

    def gather_mp(t):
        first = core * 2 * quarter_out + which * quarter_out
        return (
            remote(
                channel_in.at[pl.ds(al(part * eighth_in, eighth_in), eighth_in), pl.ds(al(t * step, step), step)],
                other_in(t, part * eighth_in, eighth_in),
                w_s.at[t, 0], w_r.at[t, 0], to_mp,
            ),
            remote(
                channel_out.at[pl.ds(al(t * step + first, 16), quarter_out), :],
                other_out(t, first, quarter_out),
                w_s.at[t, 1], w_r.at[t, 1], to_mp,
            ),
        )

    def gather_near(t):
        a = other_in(t, part * eighth_in, eighth_in)
        b = other_out(t, core * 2 * quarter_out + which * quarter_out, quarter_out)
        copies = [remote(a, a, w_s.at[t, r + 1], w_r.at[t, r + 1], near_of(r)) for r in (1, 2, 3)]
        return copies + [remote(b, b, w_s.at[t, 5], w_r.at[t, 5], to_pair)]

    def gather_core(t):
        a = other_in(t, core * 4 * eighth_in, 4 * eighth_in)
        b = other_out(t, core * 2 * quarter_out, 2 * quarter_out)
        s = lax.rem(t, 2)
        return (
            remote(a, a, wc_s.at[s, 0], wc_r.at[s, 0], to_core),
            remote(b, b, wc_s.at[s, 1], wc_r.at[s, 1], to_core),
        )

    def token_mp():
        return (
            remote(
                tw.at[core, pl.ds(0, token_half)], tw.at[core, pl.ds(token_half, token_half)], tok_s.at[0], tok_r.at[0], to_mp
            ),
        )

    def bias_mp():
        return (remote(cbs, cbo, tok_s.at[1], tok_r.at[1], to_mp),)

    def token_core():
        ref = tw.at[core, pl.ds(token_half, token_half)]
        return (remote(ref, ref, tok_s.at[2], tok_r.at[2], to_core),)

    high_bit = lax.div(line, 2)
    to_low = {"dp": dp + 4 - 8 * low}
    to_high = {"dp": dp + 8 - 16 * high_bit}

    def rows_at(first, count):
        return pl.ds(al(first, 16), count)

    def core_copy(c, h):
        slot, q, i = lax.rem(lax.div(c, 2), 2), lax.rem(c, 2), lax.rem(c, RING)
        rng = pl.ds(0, h)
        return remote(
            grads.at[slot, 1 - core, q, :, :, rng], from_core.at[slot, q, :, :, rng], c_s.at[i], c_r.at[i], to_core
        )

    def mp_copy(c, h):
        rng = pl.ds(0, h)
        return remote(acc.at[c, 1, :, rng], from_mp.at[c, :, rng], y_s.at[c], y_r.at[c], to_mp)

    def side_copy(c, h):
        rng = pl.ds(0, h)
        return remote(acc.at[c, 0, 1 - side, rng], from_x.at[c, rng], x_s.at[c], x_r.at[c], to_side)

    def both_copy(c):
        return remote(acc.at[c, :, 1 - side], from_mp.at[c], x_s.at[c], x_r.at[c], to_side)

    def then_mp_copy(c):
        return remote(acc.at[c, 1, side], from_x.at[c], y_s.at[c], y_r.at[c], to_mp)

    def low_copy(c, h):
        n = h // 2
        src = acc.at[c, 0, side, rows_at((1 - low) * n, n)]
        return remote(src, from_z.at[c, pl.ds(0, n)], z_s.at[c], z_r.at[c], to_low)

    def high_copy(c, h):
        n = h // 4
        src = acc.at[c, 0, side, rows_at(low * 2 * n + (1 - high_bit) * n, n)]
        return remote(src, from_z.at[c, pl.ds(2 * n, n)], zh_s.at[c], zh_r.at[c], to_high)

    def at_place(c, h):
        return rows_at(low * (h // 2) + high_bit * (h // 4), h // 4)

    def at_line(h, place):
        return rows_at(place * (h // 4), h // 4)

    def line_sems(c, d, first, second, third):
        return ((first.at[c], second.at[c], third.at[d])[r] for r in range(3))

    def line_copies(c, h, d):
        sends = line_sems(c, d, z_s, zh_s, zl_s)
        recvs = line_sems(c, d, z_r, zh_r, zl_r)
        return [
            remote(
                acc.at[c, 0, side, at_line(h, lax.rem(line + r, 4))],
                from_z.at[c, pl.ds((r - 1) * (h // 4), h // 4)], send, recv, line_of(r),
            )
            for r, send, recv in zip((1, 2, 3), sends, recvs)
        ]

    def keep_copy(c, rng):
        return pltpu.make_async_copy(acc.at[c, 0, side, rng], summed.at[core, c, side, rng], l_sem.at[c])

    def high_spread_copy(c, h):
        rng = at_place(c, h)
        return remote(acc.at[c, 0, side, rng], summed.at[core, c, side, rng], a_s.at[c], a_r.at[c], to_high)

    def low_spread_copy(c, h):
        ref = summed.at[core, c, side, rows_at(low * (h // 2), h // 2)]
        return remote(ref, ref, al_s.at[c], al_r.at[c], to_low)

    def spread_copies(c, h, d):
        rng = at_line(h, line)
        src, dst = acc.at[c, 0, side, rng], summed.at[core, c, side, rng]
        sends = line_sems(c, d, a_s, al_s, sl_s)
        recvs = line_sems(c, d, a_r, al_r, sl_r)
        return [remote(src, dst, send, recv, line_of(r)) for r, send, recv in zip((1, 2, 3), sends, recvs)]

    def side_spread_copy(c, h):
        ref = summed.at[core, c, side, pl.ds(0, h)]
        return remote(ref, ref, xa_s.at[c], xa_r.at[c], to_side)

    def core_spread_copy(c, h):
        ref = summed.at[core, c, :, pl.ds(0, h)]
        return remote(ref, ref, ca_s.at[c], ca_r.at[c], to_core)

    def add(a, b):
        return (a.astype(F32) + b.astype(F32)).astype(BF16)

    def core_step(c, h, send):
        core_copy(c, h).wait()
        slot, q, rng = lax.rem(lax.div(c, 2), 2), lax.rem(c, 2), pl.ds(0, h)
        acc[c, 1, :, rng] = add(grads[slot, core, q, 1, :, rng], from_core[slot, q, 1, :, rng])
        if send is mp_copy:
            send(c, h).start()
        acc[c, 0, :, rng] = add(grads[slot, core, q, 0, :, rng], from_core[slot, q, 0, :, rng])
        if send is both_copy:
            send(c).start()

    def core_mp(c, h, d):
        core_step(c, h, mp_copy)

    def core_both(c, h, d):
        core_step(c, h, both_copy)

    def mp_step(c, h, d):
        mp_copy(c, h).wait()
        rng = pl.ds(0, h)
        acc[c, 0, 1 - side, rng] = add(acc[c, 0, 1 - side, rng], from_mp[c, 1 - side, rng])
        side_copy(c, h).start()
        acc[c, 0, side, rng] = add(acc[c, 0, side, rng], from_mp[c, side, rng])

    def side_step(c, h, d):
        side_copy(c, h).wait()
        rng = pl.ds(0, h)
        acc[c, 0, side, rng] = add(acc[c, 0, side, rng], from_x[c, rng])
        low_copy(c, h).start()

    def side_line(c, h, d):
        side_copy(c, h).wait()
        rng = pl.ds(0, h)
        acc[c, 0, side, rng] = add(acc[c, 0, side, rng], from_x[c, rng])
        for copy in line_copies(c, h, d):
            copy.start()

    def both_step(c, h, d):
        both_copy(c).wait()
        acc[c, 1, side] = add(acc[c, 1, side], from_mp[c, 1])
        then_mp_copy(c).start()
        acc[c, 0, side] = add(acc[c, 0, side], from_mp[c, 0])

    def then_mp_step(c, h, d):
        then_mp_copy(c).wait()
        acc[c, 0, side] = add(acc[c, 0, side], from_x[c])
        low_copy(c, h).start()

    def low_step(c, h, d):
        low_copy(c, h).wait()
        rng = rows_at(low * (h // 2), h // 2)
        acc[c, 0, side, rng] = add(acc[c, 0, side, rng], from_z[c, pl.ds(0, h // 2)])
        high_copy(c, h).start()

    def over_far(c, rng, count):
        for i in range(len(far_bits)):
            dst = from_far.at[c, i, pl.ds(0, count)]
            copy = remote(acc.at[c, 0, side, rng], dst, far_s.at[c, i], far_r.at[c, i], far_of(i))
            copy.start()
            copy.wait()
            acc[c, 0, side, rng] = add(acc[c, 0, side, rng], from_far[c, i, pl.ds(0, count)])

    def high_step(c, h, d):
        high_copy(c, h).wait()
        rng = at_place(c, h)
        acc[c, 0, side, rng] = add(acc[c, 0, side, rng], from_z[c, pl.ds(h // 2, h // 4)])
        over_far(c, rng, h // 4)
        high_spread_copy(c, h).start()
        keep_copy(c, rng).start()

    def high_spread_step(c, h, d):
        keep_copy(c, at_place(c, h)).wait()
        high_spread_copy(c, h).wait()
        low_spread_copy(c, h).start()

    def low_spread_step(c, h, d):
        low_spread_copy(c, h).wait()
        side_spread_copy(c, h).start()

    def line_step(c, h, d):
        for copy in line_copies(c, h, d):
            copy.wait()
        rng = at_line(h, line)
        total = acc[c, 0, side, rng].astype(F32)
        for r in range(3):
            total = total + from_z[c, pl.ds(r * (h // 4), h // 4)].astype(F32)
        acc[c, 0, side, rng] = total.astype(BF16)
        over_far(c, rng, h // 4)
        for copy in spread_copies(c, h, d):
            copy.start()
        keep_copy(c, rng).start()

    def spread_step(c, h, d):
        keep_copy(c, at_line(h, line)).wait()
        for copy in spread_copies(c, h, d):
            copy.wait()
        side_spread_copy(c, h).start()

    def side_spread_step(c, h, d):
        side_spread_copy(c, h).wait()
        core_spread_copy(c, h).start()

    def core_spread_step(c, h, d):
        core_spread_copy(c, h).wait()

    steps = {
        "core_mp": core_mp, "core_both": core_both, "mp": mp_step, "side": side_step, "side_line": side_line, "both": both_step,
        "then_mp": then_mp_step, "low": low_step, "high": high_step, "high_spread": high_spread_step,
        "low_spread": low_spread_step, "line": line_step, "spread": spread_step,
        "side_spread": side_spread_step, "core_spread": core_spread_step,
    }

    def point(p, places):
        for name, entries in POINTS:
            here = [(c, at) for c, at in entries if at in places]
            if here:
                now = [(p == at).astype(jnp.int32) for _, at in here]
                c = sum(c * one for (c, _), one in zip(here, now))
                d = sum(STRAIGHT.index(c) * one for (c, _), one in zip(here, now) if c in STRAIGHT)

                @pl.when(sum(now) > 0)
                def _(c=c, d=d, name=name):
                    steps[name](c, half, d)

    barrier = pltpu.get_barrier_semaphore()
    greet = [to_mp, to_core] + [near_of(r) for r in (1, 2, 3)] + [line_of(r) for r in (1, 2, 3)]
    greet += [far_of(i) for i in range(len(far_bits))]
    for device in greet:
        pl.semaphore_signal(barrier, inc=1, device_id=device, device_id_type=MESH)

    def patch_copy(b):
        return pltpu.make_async_copy(patches.at[b], xs.at[lax.rem(b, 2)], stage_sem.at[0, lax.rem(b, 2)])

    def cot_copy(b):
        return pltpu.make_async_copy(cotangent.at[b], ms.at[lax.rem(b, 2)], stage_sem.at[1, lax.rem(b, 2)])

    def hid_save(b):
        s = lax.rem(b, 2)
        return (
            pltpu.make_async_copy(hid.at[s, pl.ds(0, 2 * token_half)], hid_out.at[b], stage_sem.at[2, s]),
            pltpu.make_async_copy(slope.at[s], slope_out.at[b], stage_sem.at[3, s]),
        )

    def hid_load(b):
        s = lax.rem(b, 2)
        return (
            pltpu.make_async_copy(hid_out.at[b], hid.at[s, pl.ds(0, 2 * token_half)], stage_sem.at[2, s]),
            pltpu.make_async_copy(slope_out.at[b], slope.at[s], stage_sem.at[3, s]),
        )

    def grad_save(b):
        return pltpu.make_async_copy(keep.at[b], inputs_grad.at[b], grad_sem.at[b])

    def mixed_save(b):
        s = lax.rem(b, 2)
        return pltpu.make_async_copy(ms.at[s], mixed.at[b], stage_sem.at[4, s])

    def both(copies, what):
        for copy in copies:
            getattr(copy, what)()

    def small_loads():
        pairs = [(token_in, tins), (token_out, touts), (token_bias, tbs), (token_shift, tss), (channel_bias, cbs.at[0])]
        vectors = (gain_one, shift_one, gain_two, shift_two, channel_shift)
        pairs += [(ref, vecs.at[i]) for i, ref in enumerate(vectors)]
        return [pltpu.make_async_copy(src, dst, small_sem.at[i]) for i, (src, dst) in enumerate(pairs)]

    both(small_loads(), "start")
    for b in (0, 1):
        patch_copy(b).start()
        cot_copy(b).start()

    wide = tw.shape[2]
    twi, two = tw.at[0], tw.at[1]

    def three(row):
        hi = row.astype(BF16).astype(F32)
        mid = (row - hi).astype(BF16).astype(F32)
        return hi, mid, row - hi - mid

    twi[pl.ds(0, token_half), :] = jnp.zeros((token_half, wide), BF16)
    two[pl.ds(0, token_half), :] = jnp.zeros((token_half, wide), BF16)
    at_row = lax.broadcasted_iota(jnp.int32, (16, wide), 0)
    at_lane = lax.broadcasted_iota(jnp.int32, (token_half, wide), 1)
    both(small_loads(), "wait")
    twi[pl.ds(0, token_half), pl.ds(0, patch)] = tins[...]
    two[pl.ds(0, token_half), pl.ds(0, patch)] = touts[...]
    padded = jnp.zeros((1, wide - token_half), F32)
    bias_row = jnp.concatenate([tbs[...].reshape(1, token_half), padded], axis=1)
    column = jnp.broadcast_to(bias_row, (LANES, wide)).T[:token_half, 0:1]
    filled = twi[pl.ds(0, token_half), :].astype(F32)
    for i, value in enumerate(three(column)):
        filled = jnp.where(at_lane == patch + i, value, filled)
    twi[pl.ds(0, token_half), :] = filled.astype(BF16)
    shift_row = jnp.concatenate([tss[...].reshape(1, patch), jnp.zeros((1, wide - patch), F32)], axis=1)
    extra = jnp.zeros((16, wide), F32)
    for i, value in enumerate(three(shift_row)):
        extra = jnp.where(at_row == i, value, extra)
    tokens = 2 * token_half
    two[pl.ds(tokens, 16), :] = extra.astype(BF16)

    pl.semaphore_wait(barrier, len(greet))
    both(token_mp(), "start")
    both(gather_mp(0), "start")
    both(bias_mp(), "start")

    def start_own(t, _):
        both(own_loads(t), "start")
        return 0

    lax.fori_loop(0, ticks, start_own, 0)

    dys[...] = jnp.zeros_like(dys)
    u2s[...] = jnp.zeros_like(u2s)
    dtok[...] = jnp.zeros_like(dtok)
    rest_rows = rows - images * high
    if rest_rows:
        chid[pl.ds(images * high, rest_rows), :] = jnp.zeros((rest_rows, chid.shape[1]), BF16)
        dcp[pl.ds(images * high, rest_rows), :] = jnp.zeros((rest_rows, dcp.shape[1]), BF16)
    row_acc[...] = jnp.zeros_like(row_acc)
    tin_acc[...] = jnp.zeros_like(tin_acc)
    tout_acc[...] = jnp.zeros_like(tout_acc)
    small[...] = jnp.zeros_like(small)
    u2s_t[pl.ds(width, 16), :] = jnp.ones((16, rows), BF16)
    for s in (0, 1):
        hid[s, pl.ds(tokens, 16), :] = jnp.ones((16, width), BF16)

    below = lax.broadcasted_iota(jnp.int32, (high, width), 0)
    ones = jnp.where(jnp.logical_and(below >= patch, below < patch + 3), 1.0, 0.0).astype(BF16)
    for b in range(images):
        u1s[b] = ones

    gain1, shift1, gain2, shift2 = (vecs[i : i + 1] for i in range(4))

    def first_norm(b, _):
        s = lax.rem(b, 2)
        patch_copy(b).wait()
        x = xs[s].astype(F32)

        @pl.when(b + 2 < images)
        def _():
            patch_copy(b + 2).start()

        keep[b] = x
        mean = jnp.mean(x, -1, keepdims=True)
        centred = x - mean
        scale = lax.rsqrt(jnp.mean(centred * centred, -1, keepdims=True) + 1e-06)
        stats[b, :, 0:1] = mean
        stats[b, :, 1:2] = scale
        u1s[b, pl.ds(0, patch), :] = (centred * scale * gain1 + shift1).astype(BF16)
        pre = dot(twi[pl.ds(0, token_half), pl.ds(0, high)], u1s[b])
        phi, deriv = gelu_parts(pre)
        at = pl.ds(al(b * token_half, 16), token_half)
        chid[at, pl.ds(0, width)] = (pre * phi).astype(BF16)
        dcp[at, pl.ds(0, width)] = deriv.astype(BF16)
        cot_copy(b).wait()
        value = ms[s]

        @pl.when(b + 2 < images)
        def _():
            cot_copy(b + 2).start()

        @pl.when(b + 1 < ticks)
        def _():
            both(gather_mp(b + 1), "start")

        @pl.when(b == images // 2)
        def _():
            both(token_mp(), "wait")
            both(token_core(), "start")

        dys[pl.ds(al(b * high, 16), patch), :] = value
        row_acc[pl.ds(4, 1), :] += jnp.sum(value.astype(F32), 0, keepdims=True)
        return 0

    lax.fori_loop(0, images, first_norm, 0)
    for t in range(images + 1, ticks):
        both(gather_mp(t), "start")

    def turn_dy(j, _):
        at = pl.ds(al(j * LANES, LANES), LANES)
        dys_t[:, at] = dys[at, :].T
        return 0

    lax.fori_loop(0, rows // LANES, turn_dy, 0)

    both(token_core(), "wait")
    two_t[...] = two[...].T

    def token_forward(b, _):
        s = lax.rem(b, 2)
        pre = dot(twi[pl.ds(token_half, token_half), pl.ds(0, high)], u1s[b])
        phi, deriv = gelu_parts(pre)

        @pl.when(b >= 2)
        def _():
            both(hid_save(b - 2), "wait")

        at = pl.ds(al(b * token_half, 16), token_half)
        hid[s, pl.ds(0, token_half), :] = chid[at, pl.ds(0, width)]
        slope[s, pl.ds(0, token_half), :] = dcp[at, pl.ds(0, width)]
        hid[s, pl.ds(token_half, token_half), :] = (pre * phi).astype(BF16)
        slope[s, pl.ds(token_half, token_half), :] = deriv.astype(BF16)
        both(hid_save(b), "start")
        x1 = keep[b] + dot(two_t[pl.ds(0, high), :], hid[s])[:patch]
        keep[b] = x1
        mean = jnp.mean(x1, -1, keepdims=True)
        centred = x1 - mean
        scale = lax.rsqrt(jnp.mean(centred * centred, -1, keepdims=True) + 1e-06)
        stats[b, :, 2:3] = mean
        stats[b, :, 3:4] = scale
        u2s[pl.ds(al(b * high, 16), patch), :] = (centred * scale * gain2 + shift2).astype(BF16)

        for t, when in enumerate((0, images // 2, images - 1)):

            @pl.when(b == when)
            def _(t=t):
                both(gather_mp(t), "wait")
                both(gather_near(t), "start")

        return 0

    lax.fori_loop(0, images, token_forward, 0)
    both(gather_near(0), "wait")
    both(gather_core(0), "start")
    both(bias_mp(), "wait")

    def turn_u2(j, _):
        at = pl.ds(al(j * LANES, LANES), LANES)
        u2s_t[pl.ds(0, width), at] = u2s[at, :].T
        return 0

    lax.fori_loop(0, rows // LANES, turn_u2, 0)
    for b in range(max(images - 2, 0), images):
        both(hid_save(b), "wait")

    live = images * high
    tiles = 2 if live % 32 == 0 else 1
    tall = live // tiles

    def channel(t, _):
        both(own_loads(t), "wait")
        both(gather_core(t), "wait")
        at = pl.ds(al(t * 2 * step, 2 * step), 2 * step)
        weight_in, weight_out = wi[:, at], wo[at, :]
        here = pl.ds(al(t * step, step), step)
        bias = jnp.concatenate([cbs[:, here], cbo[:, here]], axis=1)
        for i in range(tiles):
            rng = pl.ds(i * tall, tall)
            pre = dot(u2s[rng, :], weight_in) + bias
            back = dot_nt(dys[rng, :], weight_out)
            phi, deriv = gelu_parts(pre)
            chid[rng, at] = (pre * phi).astype(BF16)
            dcp[rng, at] = (back * deriv).astype(BF16)

        @pl.when(t + 3 < ticks)
        def _():
            both(gather_mp(t + 3), "wait")
            both(gather_near(t + 3), "start")

        @pl.when(t + 1 < ticks)
        def _():
            both(gather_near(t + 1), "wait")
            both(gather_core(t + 1), "start")

        point(2 * t, range(0, chunks, 2))
        slot = lax.rem(t, 2)
        grad_in = dot(u2s_t[...], dcp[:, at])
        cb_acc[:, at] = grad_in[width : width + 1]
        grad_in = grad_in[:width].astype(BF16)
        grad_out = dot(dys_t[...], chid[:, at]).astype(BF16)
        for m, value in ((0, grad_in), (1, grad_out)):
            for o in (0, 1):
                for q in (0, 1):
                    first = o * step + q * LANES
                    for k in (0, 1):
                        grads[slot, m, q, o, k] = value[k * half : (k + 1) * half, first : first + LANES]
        point(2 * t + 1, range(1, chunks, 2))
        core_copy(2 * t, width // 2).start()
        core_copy(2 * t + 1, width // 2).start()
        return 0

    lax.fori_loop(0, ticks, channel, 0)

    both(hid_load(0), "start")
    patch_copy(0).start()
    twi_t[...] = twi[pl.ds(0, tokens), :].T
    gain1, gain2, out_shift = vecs[0:1], vecs[2:3], vecs[4:5]

    def backward(b, _):
        s = lax.rem(b, 2)
        rng = pl.ds(al(b * high, 16), high)

        @pl.when(b + 1 < images)
        def _():
            both(hid_load(b + 1), "start")
            patch_copy(b + 1).start()

        @pl.when(b >= 2)
        def _():
            mixed_save(b - 2).wait()

        x1 = keep[b]
        ms[s] = (x1 + dot(chid[rng, :], wo[...])[:patch] + out_shift).astype(BF16)
        mixed_save(b).start()
        du2 = dot_nt(dcp[rng, :], wi[...])[:patch]
        n2 = (x1 - stats[b, :, 2:3]) * stats[b, :, 3:4]
        row_acc[pl.ds(2, 1), :] += jnp.sum(du2 * n2, 0, keepdims=True)
        row_acc[pl.ds(3, 1), :] += jnp.sum(du2, 0, keepdims=True)
        dy = dys[pl.ds(al(b * high, 16), patch), :].astype(F32)
        dx1 = dy + norm_back(du2, n2, stats[b, :, 3:4], gain2)
        keep[b] = dx1
        dtok[pl.ds(0, patch), :] = dx1.astype(BF16)
        point(chunks + 2 * b, range(chunks, chunks + 2 * images, 2))
        both(hid_load(b), "wait")
        dtk = dtok[...]
        hidden = hid[s]
        tout_acc[:, pl.ds(0, high)] += dot_nt(hidden, dtk)
        dpre = (dot(two[pl.ds(0, tokens), pl.ds(0, high)], dtk) * slope[s].astype(F32)).astype(BF16)
        tin_acc[:, pl.ds(0, high)] += dot_nt(dpre, u1s[b])
        du1 = dot(twi_t[pl.ds(0, high), :], dpre)[:patch]
        patch_copy(b).wait()
        n1 = (xs[s].astype(F32) - stats[b, :, 0:1]) * stats[b, :, 1:2]
        row_acc[pl.ds(0, 1), :] += jnp.sum(du1 * n1, 0, keepdims=True)
        row_acc[pl.ds(1, 1), :] += jnp.sum(du1, 0, keepdims=True)
        keep[b] = keep[b] + norm_back(du1, n1, stats[b, :, 1:2], gain1)
        grad_save(b).start()
        point(chunks + 2 * b + 1, range(chunks + 1, chunks + 2 * images, 2))
        return 0

    lax.fori_loop(0, images, backward, 0)

    blocks = width // LANES
    for o in (0, 1):
        for v in range(5):
            for j in range(blocks):
                small[o, pl.ds(v * blocks + j, 1), :] = row_acc[pl.ds(v, 1), pl.ds(j * LANES, LANES)]
        for j in range(2):
            small[o, pl.ds(5 * blocks + j, 1), :] = tout_acc[pl.ds(tokens, 1), pl.ds(j * LANES, LANES)]
        for c in range(chunks):
            first = (c // 2) * 2 * step + o * step + (c % 2) * LANES
            small[o, pl.ds(5 * blocks + 2 + c, 1), :] = cb_acc[pl.ds(0, 1), pl.ds(first, LANES)]
    last_slot = ticks % 2
    for o in (0, 1):
        for m, total in ((0, tin_acc), (1, tout_acc)):
            for j in range(2):
                grads[last_slot, m, 0, o, j, pl.ds(0, token_half), :] = total[
                    pl.ds(o * token_half, token_half), pl.ds(j * LANES, LANES)
                ].astype(BF16)
        grads[last_slot, 0, 0, o, 0, pl.ds(token_half, small.shape[1]), :] = small[o].astype(BF16)
    core_copy(chunks, last_half).start()
    for name, c in REST:
        steps[name](c, half if c < chunks else last_half, STRAIGHT.index(c) if c in STRAIGHT else 0)
    for b in range(max(images - 2, 0), images):
        mixed_save(b).wait()
    for b in range(images):
        grad_save(b).wait()


def widen(
    sizes, summed, mixed_in, grad_in,
    mixed, inputs_grad, d_in, d_out, d_tin, d_tbias, d_tout, d_tshift, d_gain1, d_shift1, d_gain2, d_shift2, d_cbias, d_cshift,
    sums, last, wide_in, wide_out, hold_mixed, hold_grad, in_sem, out_sem, last_sem, through_sem,
):
    images, patch, width, token_half, chunks = sizes

    def at(c):
        return pl.ds(c * LANES, LANES)

    loads = [[pltpu.make_async_copy(summed.at[m, c], sums.at[m, c], in_sem.at[m, c]) for m in (0, 1)] for c in range(chunks)]
    stores = [
        (
            pltpu.make_async_copy(wide_in.at[:, at(c)], d_in.at[:, at(c)], out_sem.at[0, c]),
            pltpu.make_async_copy(wide_out.at[at(c)], d_out.at[at(c)], out_sem.at[1, c]),
        )
        for c in range(chunks)
    ]
    load_last = [
        pltpu.make_async_copy(summed.at[m, chunks, :, pl.ds(0, last.shape[2])], last.at[m], last_sem.at[m]) for m in (0, 1)
    ]
    ins, outs = [], []
    for i, (src, hold, dst) in enumerate(((mixed_in, hold_mixed, mixed), (grad_in, hold_grad, inputs_grad))):
        for b in range(images):
            ins.append(pltpu.make_async_copy(src.at[b], hold.at[b], through_sem.at[i, b]))
            outs.append(pltpu.make_async_copy(hold.at[b], dst.at[b], through_sem.at[i + 2, b]))
    for pair in loads:
        for copy in pair:
            copy.start()
    for copy in load_last + ins:
        copy.start()
    through = iter(zip(ins, outs))
    for c in range(chunks):
        for copy in loads[c]:
            copy.wait()
        wide_in[:, c * LANES : (c + 1) * LANES] = sums[0, c].reshape(width, LANES).astype(F32)
        stores[c][0].start()
        wide_out[c * LANES : (c + 1) * LANES, :] = sums[1, c].reshape(width, LANES).T.astype(F32)
        stores[c][1].start()
        for arrived, leave in [pair for pair in (next(through, None),) if pair]:
            arrived.wait()
            leave.start()
    for arrived, leave in through:
        arrived.wait()
        leave.start()
    for copy in load_last:
        copy.wait()

    def token_block(m):
        halves = [last[m, j, pl.ds(0, token_half), :] for j in (0, 1)]
        return jnp.concatenate(halves, axis=1).astype(F32)

    grad = token_block(0)
    d_tin[...] = grad[:, :patch]
    d_tbias[...] = grad.T[patch : patch + 1].reshape(token_half)
    d_tout[...] = token_block(1)[:, :patch]
    blocks = width // LANES
    rows = last[0, 0, pl.ds(token_half, 64), :].astype(F32)

    def vector(first, count):
        return jnp.concatenate([rows[first + j : first + j + 1] for j in range(count)], axis=1)

    for v, ref in enumerate((d_gain1, d_shift1, d_gain2, d_shift2, d_cshift)):
        ref[...] = vector(v * blocks, blocks).reshape(width)
    d_tshift[...] = vector(5 * blocks, 2)[:, :patch].reshape(patch)
    d_cbias[...] = vector(5 * blocks + 2, chunks).reshape(chunks * LANES)
    for pair in stores:
        for copy in pair:
            copy.wait()
    for copy in outs:
        copy.wait()


def per_device(
    dp_size,
    patches, cotangent, gain_one, shift_one, token_in, token_bias, token_out, token_shift,
    gain_two, shift_two, channel_in, channel_bias, channel_out, channel_shift,
):
    images, patch, width = patches.shape
    token_half = token_in.shape[1]
    hidden_half = channel_in.shape[1]
    step = 2 * LANES
    ticks = hidden_half // step
    chunks = 2 * ticks
    high = -(-(patch + 3) // 16) * 16
    rows = -(-images * high // LANES) * LANES
    wide = -(-patch // LANES) * LANES
    tokens = 2 * token_half
    far = max(sum(1 for b in range(4, 20) if 2**b < dp_size), 1)
    far_chunks = chunks + 1 if dp_size > 16 else 1
    last_half = -(-(token_half + 64) // 64) * 64
    sizes = (images, patch, width, token_half, hidden_half, ticks, dp_size, last_half)
    hbm = pl.BlockSpec(memory_space=pl.ANY)
    n = chunks + 1
    half = width // 2
    dma = pltpu.SemaphoreType.DMA
    mixed, inputs_grad, summed, _, _ = pl.pallas_call(
        functools.partial(layer, sizes),
        out_shape=(
            jax.ShapeDtypeStruct((images, patch, width), BF16),
            jax.ShapeDtypeStruct((images, patch, width), F32),
            jax.ShapeDtypeStruct((2, n, 2, half, LANES), BF16),
            jax.ShapeDtypeStruct((images, tokens, width), BF16),
            jax.ShapeDtypeStruct((images, tokens, width), BF16),
        ),
        in_specs=[hbm] * 14,
        out_specs=(hbm,) * 5,
        scratch_shapes=[
            pltpu.VMEM((width, 2 * hidden_half), BF16),
            pltpu.VMEM((2 * hidden_half, width), BF16),
            pltpu.VMEM((8, width), F32),
            pltpu.VMEM((1, hidden_half), F32),
            pltpu.VMEM((1, hidden_half), F32),
            pltpu.VMEM((token_half,), F32),
            pltpu.VMEM((patch,), F32),
            pltpu.VMEM((token_half, patch), BF16),
            pltpu.VMEM((token_half, patch), BF16),
            pltpu.VMEM((2, tokens + 16, wide), BF16),
            pltpu.VMEM((wide, tokens), BF16),
            pltpu.VMEM((wide, tokens + 16), BF16),
            pltpu.VMEM((images, patch, width), F32),
            pltpu.VMEM((rows, width), BF16),
            pltpu.VMEM((width, rows), BF16),
            pltpu.VMEM((rows, width), BF16),
            pltpu.VMEM((width + 16, rows), BF16),
            pltpu.VMEM((images, high, width), BF16),
            pltpu.VMEM((rows, 2 * hidden_half), BF16),
            pltpu.VMEM((rows, 2 * hidden_half), BF16),
            pltpu.VMEM((high, width), BF16),
            pltpu.VMEM((2, patch, width), BF16),
            pltpu.VMEM((2, patch, width), BF16),
            pltpu.VMEM((2, tokens + 16, width), BF16),
            pltpu.VMEM((2, tokens, width), BF16),
            pltpu.VMEM((images, patch, 4), F32),
            pltpu.VMEM((8, width), F32),
            pltpu.VMEM((1, 2 * hidden_half), F32),
            pltpu.VMEM((tokens, wide), F32),
            pltpu.VMEM((tokens + 16, wide), F32),
            pltpu.VMEM((2, 64, LANES), F32),
            pltpu.VMEM((2, 2, 2, 2, 2, half, LANES), BF16),
            pltpu.VMEM((2, 2, 2, 2, half, LANES), BF16),
            pltpu.VMEM((n, 2, 2, half, LANES), BF16),
            pltpu.VMEM((n, 2, half, LANES), BF16),
            pltpu.VMEM((n, half, LANES), BF16),
            pltpu.VMEM((n, 3 * (half // 4), LANES), BF16),
            pltpu.VMEM((far_chunks, far, half // 4, LANES), BF16),
            dma((ticks, 2)),
            dma((5, 2)),
            dma((10,)),
            dma((images,)),
            dma((3,)), dma((3,)),
            dma((ticks, 6)), dma((ticks, 6)),
            dma((2, 2)), dma((2, 2)),
            dma((RING,)), dma((RING,)),
            dma((n,)), dma((n,)),
            dma((n,)), dma((n,)),
            dma((n,)), dma((n,)),
            dma((n,)), dma((n,)),
            dma((len(STRAIGHT),)), dma((len(STRAIGHT),)),
            dma((n,)), dma((n,)),
            dma((n,)), dma((n,)),
            dma((len(STRAIGHT),)), dma((len(STRAIGHT),)),
            dma((n,)),
            dma((n,)), dma((n,)),
            dma((n,)), dma((n,)),
            dma((far_chunks, far)), dma((far_chunks, far)),
        ],
        compiler_params=pltpu.CompilerParams(
            collective_id=0, has_side_effects=True, vmem_limit_bytes=63 * 2**20
        ),
        name="mixer_layer",
    )(
        patches, cotangent, gain_one, shift_one, token_in.T, token_bias, token_out, token_shift,
        gain_two, shift_two, channel_in, channel_bias, channel_out, channel_shift,
    )

    vmem = pl.BlockSpec(memory_space=pltpu.VMEM)
    shapes = (
        (token_half, patch), (token_half,), (token_half, patch), (patch,),
        (width,), (width,), (width,), (width,), (hidden_half,), (width,),
    )
    (
        mixed, inputs_grad, d_in, d_out, d_tin, d_tbias, d_tout, d_tshift,
        d_gain1, d_shift1, d_gain2, d_shift2, d_cbias, d_cshift,
    ) = pl.pallas_call(
        functools.partial(widen, (images, patch, width, token_half, chunks)),
        in_specs=[hbm] * 3,
        out_specs=(hbm,) * 4 + (vmem,) * len(shapes),
        out_shape=(
            jax.ShapeDtypeStruct((images, patch, width), BF16),
            jax.ShapeDtypeStruct((images, patch, width), F32),
            jax.ShapeDtypeStruct((width, hidden_half), F32),
            jax.ShapeDtypeStruct((hidden_half, width), F32),
        ) + tuple(jax.ShapeDtypeStruct(shape, F32) for shape in shapes),
        scratch_shapes=[
            pltpu.VMEM((2, chunks, 2, half, LANES), BF16),
            pltpu.VMEM((2, 2, last_half, LANES), BF16),
            pltpu.VMEM((width, hidden_half), F32),
            pltpu.VMEM((hidden_half, width), F32),
            pltpu.VMEM((images, patch, width), BF16),
            pltpu.VMEM((images, patch, width), F32),
            dma((2, chunks)), dma((2, chunks)), dma((2,)), dma((4, images)),
        ],
        compiler_params=pltpu.CompilerParams(vmem_limit_bytes=60 * 2**20),
        name="widen",
    )(summed, mixed, inputs_grad)
    return (
        mixed, inputs_grad, d_gain1, d_shift1, d_tin.T, d_tbias, d_tout, d_tshift,
        d_gain2, d_shift2, d_in, d_cbias, d_out, d_cshift,
    )


def solution(mesh):
    split = P(("dp", "mp"), None, None)
    columns, rows, vector = P(None, "mp"), P("mp", None), P("mp")
    return jax.shard_map(
        functools.partial(per_device, mesh.shape["dp"]),
        mesh=mesh,
        in_specs=(
            split, split, P(), P(), columns, vector, rows, P(), P(), P(), columns, vector, rows, P(),
        ),
        out_specs=(
            split, split, P(), P(), columns, vector, rows, P(), P(), P(), columns, vector, rows, P(),
        ),
        check_vma=False,
    )
```

time: 157 us -> 126 us (0.80)
  local copies, waits for them, and re-layouts: 20.6 us -> 0 us
  Pallas kernels: 135 us -> 125 us
    pallas_call x1, Pallas kernels: 128 us -> 115 us  [per_device(): pl.pallas_call(functools.partial(layer, sizes), out_shape=(jax.ShapeDtype...]
    reshape x8 -> x0, local copies, waits for them, and re-layouts: 10.5 us -> none  [the longest x1 1.44 us: per_device(): token_shift.reshape(-1, 1)]
    unnamed x10 -> x0, local copies, waits for them, and re-layouts: 9.43 us -> none
    pallas_call x1, Pallas kernels: 6.73 us -> 10.4 us  [per_device(): pl.pallas_call(functools.partial(widen, (images, patch, width, token_half...]
where the time goes in v2:
time: 126 us
  Pallas kernels  125 us (99%)
    pallas_call x1, Pallas kernels, per_device(): pl.pallas_call(functools.partial(layer, sizes), out_shape=(jax.ShapeDtype...  115 us
    pallas_call x1, Pallas kernels, per_device(): pl.pallas_call(functools.partial(widen, (images, patch, width, token_half...  10.4 us

profile of v2, /device:TPU:0, one launch (start us, length us, event | category | flops | bytes accessed | tf_op | source)
XLA Modules:
  0.0 126.1 jit_solution(872509166942964454)
XLA Ops:
  0.7 114.9 %mixer_layer.1 = (bf16[6,196,768]{2,1,0:T(8,128)(2,1)}, f32[6,196,768]{2,1,0:T(8,128)}, bf16[2,13,2,384,128]{4,3,2,1,0:T(8,128)(2,1)}, bf16[6,384,768]{2,1,0:T(8,128)(2,1)}, bf16[6,384,768]{2,1,0:T(8,128)(2,1)}) custom-call(bf16[6,196,768]{2,1,0:T(8,128)(2,1)} %patches.1, bf16[6,196,768]{2,1,0:T(8,128)(2,1)} %cotangent.1, f32[768]{0:T(1024)} %gain_one.1, ...), custom_call_target="tpu_custom_call" | custom-call | tf_op jit(solution)/shard_map/mixer_layer/pallas_call | solution.py:840
  115.5 10.4 %widen.1 = (bf16[6,196,768]{2,1,0:T(8,128)(2,1)}, f32[6,196,768]{2,1,0:T(8,128)}, f32[768,1536]{1,0:T(8,128)}, f32[1536,768]{1,0:T(8,128)}, f32[192,196]{1,0:T(8...) custom-call(bf16[2,13,2,384,128]{4,3,2,1,0:T(8,128)(2,1)} %get-tuple, ...), custom_call_target="tpu_custom_call" | custom-call | tf_op jit(solution)/shard_map/widen/pallas_call | solution.py:928

commit v3 on v2

--- a/solution.py
+++ b/solution.py
@@ -14,32 +14,33 @@
 LANES = 128
 RING = 4
 
-STRAIGHT = (0, 2, 3, 5, 6, 10, 12)
+STRAIGHT = (0, 2, 4, 8, 11, 12)
 POINTS = (
-    ("core_mp", ((0, 2), (2, 4), (3, 5), (5, 7), (6, 8), (7, 9), (8, 10), (9, 11), (10, 12))),
-    ("core_both", ((1, 3), (4, 6), (11, 13))),
-    ("mp", ((0, 6), (2, 8), (3, 10), (5, 12), (6, 14), (7, 16), (8, 18), (9, 20), (10, 22))),
-    ("both", ((1, 7), (4, 10), (11, 16))),
-    ("side", ((7, 18), (8, 20), (9, 23))),
-    ("side_line", ((0, 11), (2, 12), (3, 13), (5, 14), (6, 17))),
-    ("then_mp", ((1, 12), (4, 18), (11, 23))),
-    ("low", ((1, 14), (7, 20), (4, 21), (8, 22))),
-    ("high", ((1, 18), (7, 22), (4, 23))),
-    ("line", ((0, 13), (2, 14), (3, 15), (5, 17), (6, 20))),
-    ("high_spread", ((1, 22),)),
-    ("spread", ((0, 16), (2, 18), (3, 20), (5, 21), (6, 23))),
-    ("side_spread", ((0, 19), (2, 21), (3, 22))),
-    ("core_spread", ((0, 20), (2, 22), (3, 23))),
+    ("core_mp", ((0, 2), (2, 4), (3, 5), (4, 6), (5, 7), (6, 8), (8, 10), (9, 11), (11, 13))),
+    ("core_both", ((1, 3), (7, 9), (10, 12))),
+    ("mp", ((0, 6), (2, 8), (3, 10), (4, 12), (5, 13), (6, 16), (8, 17), (9, 19), (11, 22))),
+    ("both", ((1, 7), (7, 12), (10, 15))),
+    ("side", ((3, 13), (5, 17), (6, 18), (9, 21))),
+    ("side_line", ((0, 10), (2, 11), (4, 16), (8, 20))),
+    ("then_mp", ((1, 14), (7, 20), (10, 22))),
+    ("low", ((3, 15), (1, 16), (5, 19), (6, 20), (7, 22), (9, 23))),
+    ("high", ((3, 17), (1, 19), (5, 21), (6, 23))),
+    ("line", ((0, 13), (2, 14), (4, 18), (8, 22))),
+    ("high_spread", ((3, 19), (1, 21), (5, 23))),
+    ("low_spread", ((3, 21),)),
+    ("spread", ((0, 15), (2, 16), (4, 20))),
+    ("side_spread", ((0, 18), (2, 19), (4, 22), (3, 23))),
+    ("core_spread", ((0, 19), (2, 20), (4, 23))),
 )
 REST = (
-    ("low_spread", 1), ("side_spread", 5), ("high_spread", 7), ("core_mp", 12), ("high", 8), ("core_spread", 5),
-    ("low", 11), ("side_line", 10), ("low", 9), ("high_spread", 4), ("side_spread", 6), ("low_spread", 7),
-    ("high_spread", 8), ("mp", 12), ("core_spread", 6), ("high", 11), ("side_spread", 1), ("line", 10),
-    ("core_spread", 1), ("side_spread", 7), ("low_spread", 4), ("high", 9), ("low_spread", 8), ("core_spread", 7),
-    ("side_line", 12), ("high_spread", 11), ("spread", 10), ("side_spread", 4), ("high_spread", 9),
-    ("core_spread", 4), ("low_spread", 11), ("line", 12), ("side_spread", 8), ("low_spread", 9), ("core_spread", 8),
-    ("side_spread", 10), ("spread", 12), ("core_spread", 10), ("side_spread", 11), ("core_spread", 11),
-    ("side_spread", 9), ("core_spread", 9), ("side_spread", 12), ("core_spread", 12),
+    ("low_spread", 1), ("core_spread", 3), ("high", 7), ("side_line", 11), ("core_mp", 12), ("low", 10),
+    ("spread", 8), ("high_spread", 6), ("side_spread", 1), ("low_spread", 5), ("high", 9), ("core_spread", 1),
+    ("high_spread", 7), ("mp", 12), ("side_spread", 8), ("line", 11), ("core_spread", 8), ("low_spread", 6),
+    ("high", 10), ("side_spread", 5), ("high_spread", 9), ("low_spread", 7), ("core_spread", 5), ("side_line", 12),
+    ("spread", 11), ("side_spread", 6), ("high_spread", 10), ("low_spread", 9), ("core_spread", 6), ("line", 12),
+    ("side_spread", 7), ("core_spread", 7), ("low_spread", 10), ("side_spread", 11), ("core_spread", 11),
+    ("spread", 12), ("side_spread", 9), ("core_spread", 9), ("side_spread", 10), ("core_spread", 10),
+    ("side_spread", 12), ("core_spread", 12),
 )
 
 
@@ -80,8 +81,8 @@
     xs, ms, hid, slope, stats,
     row_acc, cb_acc, tin_acc, tout_acc, small,
     grads, from_core, acc, from_mp, from_x, from_z, from_far,
-    load_sem, stage_sem, small_sem, grad_sem, tok_s, tok_r, w_s, w_r, wc_s, wc_r, c_s, c_r, y_s, y_r, x_s, x_r, z_s, z_r, zh_s, zh_r, zl_s, zl_r,
-    a_s, a_r, al_s, al_r, sl_s, sl_r, l_sem, xa_s, xa_r, ca_s, ca_r, far_s, far_r,
+    load_sem, stage_sem, small_sem, grad_sem, tok_s, tok_r, w_s, w_r, wc_s, wc_r, c_s, c_r, g_s, line_s, l_sem, y_r, x_r, z_r, zh_r, zl_r,
+    a_r, al_r, sl_r, xa_r, ca_r, far_s, far_r, hello,
 ):
     images, patch, width, token_half, hidden_half, ticks, dp_size, last_half = sizes
     rows = dys.shape[0]
@@ -170,8 +171,8 @@
     def gather_near(t):
         a = other_in(t, part * eighth_in, eighth_in)
         b = other_out(t, core * 2 * quarter_out + which * quarter_out, quarter_out)
-        copies = [remote(a, a, w_s.at[t, r + 1], w_r.at[t, r + 1], near_of(r)) for r in (1, 2, 3)]
-        return copies + [remote(b, b, w_s.at[t, 5], w_r.at[t, 5], to_pair)]
+        copies = [remote(a, a, w_s.at[t, r - 1], w_r.at[t, r + 1], near_of(r)) for r in (1, 2, 3)]
+        return copies + [remote(b, b, w_s.at[t, 3], w_r.at[t, 5], to_pair)]
 
     def gather_core(t):
         a = other_in(t, core * 4 * eighth_in, 4 * eighth_in)
@@ -212,27 +213,27 @@
 
     def mp_copy(c, h):
         rng = pl.ds(0, h)
-        return remote(acc.at[c, 1, :, rng], from_mp.at[c, :, rng], y_s.at[c], y_r.at[c], to_mp)
+        return remote(acc.at[c, 1, :, rng], from_mp.at[c, :, rng], g_s.at[0, c], y_r.at[c], to_mp)
 
     def side_copy(c, h):
         rng = pl.ds(0, h)
-        return remote(acc.at[c, 0, 1 - side, rng], from_x.at[c, rng], x_s.at[c], x_r.at[c], to_side)
+        return remote(acc.at[c, 0, 1 - side, rng], from_x.at[c, rng], g_s.at[0, c], x_r.at[c], to_side)
 
     def both_copy(c):
-        return remote(acc.at[c, :, 1 - side], from_mp.at[c], x_s.at[c], x_r.at[c], to_side)
+        return remote(acc.at[c, :, 1 - side], from_mp.at[c], g_s.at[0, c], x_r.at[c], to_side)
 
     def then_mp_copy(c):
-        return remote(acc.at[c, 1, side], from_x.at[c], y_s.at[c], y_r.at[c], to_mp)
+        return remote(acc.at[c, 1, side], from_x.at[c], g_s.at[0, c], y_r.at[c], to_mp)
 
     def low_copy(c, h):
         n = h // 2
         src = acc.at[c, 0, side, rows_at((1 - low) * n, n)]
-        return remote(src, from_z.at[c, pl.ds(0, n)], z_s.at[c], z_r.at[c], to_low)
+        return remote(src, from_z.at[c, pl.ds(0, n)], g_s.at[0, c], z_r.at[c], to_low)
 
     def high_copy(c, h):
         n = h // 4
         src = acc.at[c, 0, side, rows_at(low * 2 * n + (1 - high_bit) * n, n)]
-        return remote(src, from_z.at[c, pl.ds(2 * n, n)], zh_s.at[c], zh_r.at[c], to_high)
+        return remote(src, from_z.at[c, pl.ds(2 * n, n)], g_s.at[0, c], zh_r.at[c], to_high)
 
     def at_place(c, h):
         return rows_at(low * (h // 2) + high_bit * (h // 4), h // 4)
@@ -244,7 +245,7 @@
         return ((first.at[c], second.at[c], third.at[d])[r] for r in range(3))
 
     def line_copies(c, h, d):
-        sends = line_sems(c, d, z_s, zh_s, zl_s)
+        sends = line_sems(c, d, g_s.at[0], g_s.at[1], line_s)
         recvs = line_sems(c, d, z_r, zh_r, zl_r)
         return [
             remote(
@@ -254,31 +255,38 @@
             for r, send, recv in zip((1, 2, 3), sends, recvs)
         ]
 
-    def keep_copy(c, rng):
-        return pltpu.make_async_copy(acc.at[c, 0, side, rng], summed.at[core, c, side, rng], l_sem.at[c])
+    def sums_of(c, rng):
+        return from_mp.at[c, 0, rng]
+
+    def keep_copy(c, h):
+        rng = pl.ds(0, h)
+        return pltpu.make_async_copy(sums_of(c, rng), summed.at[core, c, side, rng], l_sem.at[c])
 
     def high_spread_copy(c, h):
-        rng = at_place(c, h)
-        return remote(acc.at[c, 0, side, rng], summed.at[core, c, side, rng], a_s.at[c], a_r.at[c], to_high)
+        ref = sums_of(c, at_place(c, h))
+        return remote(ref, ref, g_s.at[0, c], a_r.at[c], to_high)
 
     def low_spread_copy(c, h):
-        ref = summed.at[core, c, side, rows_at(low * (h // 2), h // 2)]
-        return remote(ref, ref, al_s.at[c], al_r.at[c], to_low)
+        ref = sums_of(c, rows_at(low * (h // 2), h // 2))
+        return remote(ref, ref, g_s.at[0, c], al_r.at[c], to_low)
 
     def spread_copies(c, h, d):
-        rng = at_line(h, line)
-        src, dst = acc.at[c, 0, side, rng], summed.at[core, c, side, rng]
-        sends = line_sems(c, d, a_s, al_s, sl_s)
+        ref = sums_of(c, at_line(h, line))
+        sends = line_sems(c, d, g_s.at[0], g_s.at[1], line_s)
         recvs = line_sems(c, d, a_r, al_r, sl_r)
-        return [remote(src, dst, send, recv, line_of(r)) for r, send, recv in zip((1, 2, 3), sends, recvs)]
+        return [remote(ref, ref, send, recv, line_of(r)) for r, send, recv in zip((1, 2, 3), sends, recvs)]
 
     def side_spread_copy(c, h):
-        ref = summed.at[core, c, side, pl.ds(0, h)]
-        return remote(ref, ref, xa_s.at[c], xa_r.at[c], to_side)
-
-    def core_spread_copy(c, h):
-        ref = summed.at[core, c, :, pl.ds(0, h)]
-        return remote(ref, ref, ca_s.at[c], ca_r.at[c], to_core)
+        rng = pl.ds(0, h)
+        return remote(sums_of(c, rng), summed.at[core, c, side, rng], g_s.at[0, c], xa_r.at[c], to_side)
+
+    def core_own_copy(c, h):
+        rng = pl.ds(0, h)
+        return remote(sums_of(c, rng), summed.at[core, c, side, rng], g_s.at[1, c], ca_r.at[0, c], to_core)
+
+    def core_other_copy(c, h):
+        ref = summed.at[core, c, 1 - side, pl.ds(0, h)]
+        return remote(ref, ref, g_s.at[0, c], ca_r.at[1, c], to_core)
 
     def add(a, b):
         return (a.astype(F32) + b.astype(F32)).astype(BF16)
@@ -339,27 +347,27 @@
     def over_far(c, rng, count):
         for i in range(len(far_bits)):
             dst = from_far.at[c, i, pl.ds(0, count)]
-            copy = remote(acc.at[c, 0, side, rng], dst, far_s.at[c, i], far_r.at[c, i], far_of(i))
+            copy = remote(sums_of(c, rng), dst, far_s.at[c, i], far_r.at[c, i], far_of(i))
             copy.start()
             copy.wait()
-            acc[c, 0, side, rng] = add(acc[c, 0, side, rng], from_far[c, i, pl.ds(0, count)])
+            from_mp[c, 0, rng] = add(from_mp[c, 0, rng], from_far[c, i, pl.ds(0, count)])
 
     def high_step(c, h, d):
         high_copy(c, h).wait()
         rng = at_place(c, h)
-        acc[c, 0, side, rng] = add(acc[c, 0, side, rng], from_z[c, pl.ds(h // 2, h // 4)])
+        from_mp[c, 0, rng] = add(acc[c, 0, side, rng], from_z[c, pl.ds(h // 2, h // 4)])
         over_far(c, rng, h // 4)
         high_spread_copy(c, h).start()
-        keep_copy(c, rng).start()
 
     def high_spread_step(c, h, d):
-        keep_copy(c, at_place(c, h)).wait()
         high_spread_copy(c, h).wait()
         low_spread_copy(c, h).start()
 
     def low_spread_step(c, h, d):
         low_spread_copy(c, h).wait()
         side_spread_copy(c, h).start()
+        core_own_copy(c, h).start()
+        keep_copy(c, h).start()
 
     def line_step(c, h, d):
         for copy in line_copies(c, h, d):
@@ -368,24 +376,26 @@
         total = acc[c, 0, side, rng].astype(F32)
         for r in range(3):
             total = total + from_z[c, pl.ds(r * (h // 4), h // 4)].astype(F32)
-        acc[c, 0, side, rng] = total.astype(BF16)
+        from_mp[c, 0, rng] = total.astype(BF16)
         over_far(c, rng, h // 4)
         for copy in spread_copies(c, h, d):
             copy.start()
-        keep_copy(c, rng).start()
 
     def spread_step(c, h, d):
-        keep_copy(c, at_line(h, line)).wait()
         for copy in spread_copies(c, h, d):
             copy.wait()
         side_spread_copy(c, h).start()
+        core_own_copy(c, h).start()
+        keep_copy(c, h).start()
 
     def side_spread_step(c, h, d):
         side_spread_copy(c, h).wait()
-        core_spread_copy(c, h).start()
+        core_other_copy(c, h).start()
 
     def core_spread_step(c, h, d):
-        core_spread_copy(c, h).wait()
+        core_own_copy(c, h).wait()
+        keep_copy(c, h).wait()
+        core_other_copy(c, h).wait()
 
     steps = {
         "core_mp": core_mp, "core_both": core_both, "mp": mp_step, "side": side_step, "side_line": side_line, "both": both_step,
@@ -407,10 +417,40 @@
                     steps[name](c, half, d)
 
     barrier = pltpu.get_barrier_semaphore()
-    greet = [to_mp, to_core] + [near_of(r) for r in (1, 2, 3)] + [line_of(r) for r in (1, 2, 3)]
-    greet += [far_of(i) for i in range(len(far_bits))]
+    to_mid = {"dp": dp + 4 * (3 - 2 * line)}
+    is_mid = lax.rem(lax.div(line + 1, 2), 2)
+    greet = [to_mp, to_core, to_side, to_low] + [far_of(i) for i in range(len(far_bits))]
     for device in greet:
         pl.semaphore_signal(barrier, inc=1, device_id=device, device_id_type=MESH)
+
+    @pl.when(is_mid == 1)
+    def _():
+        pl.semaphore_signal(barrier, inc=1, device_id=to_mid, device_id_type=MESH)
+
+    def tell(i, device):
+        pl.semaphore_signal(hello.at[i], inc=1, device_id=device, device_id_type=MESH)
+
+    def first_word():
+        tell(0, to_side)
+        tell(1, to_low)
+
+        @pl.when(is_mid == 1)
+        def _():
+            tell(2, to_mid)
+
+    def second_word():
+        for i in (0, 1):
+            pl.semaphore_wait(hello.at[i], 1)
+
+        @pl.when(is_mid == 1)
+        def _():
+            pl.semaphore_wait(hello.at[2], 1)
+
+        tell(3, to_low)
+
+    def last_word():
+        pl.semaphore_wait(hello.at[3], 1)
+
 
     def patch_copy(b):
         return pltpu.make_async_copy(patches.at[b], xs.at[lax.rem(b, 2)], stage_sem.at[0, lax.rem(b, 2)])
@@ -483,9 +523,10 @@
     tokens = 2 * token_half
     two[pl.ds(tokens, 16), :] = extra.astype(BF16)
 
-    pl.semaphore_wait(barrier, len(greet))
+    pl.semaphore_wait(barrier, len(greet) + is_mid)
     both(token_mp(), "start")
     both(gather_mp(0), "start")
+    first_word()
     both(bias_mp(), "start")
 
     def start_own(t, _):
@@ -568,6 +609,7 @@
 
     lax.fori_loop(0, rows // LANES, turn_dy, 0)
 
+    second_word()
     both(token_core(), "wait")
     two_t[...] = two[...].T
 
@@ -608,6 +650,7 @@
     both(gather_near(0), "wait")
     both(gather_core(0), "start")
     both(bias_mp(), "wait")
+    last_word()
 
     def turn_u2(j, _):
         at = pl.ds(al(j * LANES, LANES), LANES)
@@ -892,21 +935,14 @@
             dma((10,)),
             dma((images,)),
             dma((3,)), dma((3,)),
-            dma((ticks, 6)), dma((ticks, 6)),
+            dma((ticks, 4)), dma((ticks, 6)),
             dma((2, 2)), dma((2, 2)),
             dma((RING,)), dma((RING,)),
-            dma((n,)), dma((n,)),
-            dma((n,)), dma((n,)),
-            dma((n,)), dma((n,)),
-            dma((n,)), dma((n,)),
-            dma((len(STRAIGHT),)), dma((len(STRAIGHT),)),
-            dma((n,)), dma((n,)),
-            dma((n,)), dma((n,)),
-            dma((len(STRAIGHT),)), dma((len(STRAIGHT),)),
-            dma((n,)),
-            dma((n,)), dma((n,)),
-            dma((n,)), dma((n,)),
+            dma((2, n)), dma((len(STRAIGHT),)), dma((n,)),
+            dma((n,)), dma((n,)), dma((n,)), dma((n,)), dma((len(STRAIGHT),)),
+            dma((n,)), dma((n,)), dma((len(STRAIGHT),)), dma((n,)), dma((2, n)),
             dma((far_chunks, far)), dma((far_chunks, far)),
+            pltpu.SemaphoreType.REGULAR((4,)),
         ],
         compiler_params=pltpu.CompilerParams(
             collective_id=0, has_side_effects=True, vmem_limit_bytes=63 * 2**20

time: 126 us -> 122 us (0.968)
  Pallas kernels: 125 us -> 121 us
    pallas_call x1, Pallas kernels: 115 us -> 110 us  [per_device(): pl.pallas_call(functools.partial(layer, sizes), out_shape=(jax.ShapeDtype...]
where the time goes in v3:
time: 122 us
  Pallas kernels  121 us (99%)
    pallas_call x1, Pallas kernels, per_device(): pl.pallas_call(functools.partial(layer, sizes), out_shape=(jax.ShapeDtype...  110 us
    pallas_call x1, Pallas kernels, per_device(): pl.pallas_call(functools.partial(widen, (images, patch, width, token_half...  10.4 us

profile of v3, /device:TPU:0, one launch (start us, length us, event | category | flops | bytes accessed | tf_op | source)
XLA Modules:
  0.0 121.6 jit_solution(787535601043060322)
XLA Ops:
  0.7 110.3 %mixer_layer.1 = (bf16[6,196,768]{2,1,0:T(8,128)(2,1)}, f32[6,196,768]{2,1,0:T(8,128)}, bf16[2,13,2,384,128]{4,3,2,1,0:T(8,128)(2,1)}, bf16[6,384,768]{2,1,0:T(8,128)(2,1)}, bf16[6,384,768]{2,1,0:T(8,128)(2,1)}) custom-call(bf16[6,196,768]{2,1,0:T(8,128)(2,1)} %patches.1, bf16[6,196,768]{2,1,0:T(8,128)(2,1)} %cotangent.1, f32[768]{0:T(1024)} %gain_one.1, ...), custom_call_target="tpu_custom_call" | custom-call | tf_op jit(solution)/shard_map/mixer_layer/pallas_call | solution.py:883
  111.0 10.4 %widen.1 = (bf16[6,196,768]{2,1,0:T(8,128)(2,1)}, f32[6,196,768]{2,1,0:T(8,128)}, f32[768,1536]{1,0:T(8,128)}, f32[1536,768]{1,0:T(8,128)}, f32[192,196]{1,0:T(8...) custom-call(bf16[2,13,2,384,128]{4,3,2,1,0:T(8,128)(2,1)} %get-tuple, ...), custom_call_target="tpu_custom_call" | custom-call | tf_op jit(solution)/shard_map/widen/pallas_call | solution.py:964

commit v4 on v3

--- a/solution.py
+++ b/solution.py
@@ -14,33 +14,33 @@
 LANES = 128
 RING = 4
 
-STRAIGHT = (0, 2, 4, 8, 11, 12)
+STRAIGHT = (4, 5, 8, 9, 11, 12)
 POINTS = (
     ("core_mp", ((0, 2), (2, 4), (3, 5), (4, 6), (5, 7), (6, 8), (8, 10), (9, 11), (11, 13))),
     ("core_both", ((1, 3), (7, 9), (10, 12))),
-    ("mp", ((0, 6), (2, 8), (3, 10), (4, 12), (5, 13), (6, 16), (8, 17), (9, 19), (11, 22))),
-    ("both", ((1, 7), (7, 12), (10, 15))),
-    ("side", ((3, 13), (5, 17), (6, 18), (9, 21))),
-    ("side_line", ((0, 10), (2, 11), (4, 16), (8, 20))),
-    ("then_mp", ((1, 14), (7, 20), (10, 22))),
-    ("low", ((3, 15), (1, 16), (5, 19), (6, 20), (7, 22), (9, 23))),
-    ("high", ((3, 17), (1, 19), (5, 21), (6, 23))),
-    ("line", ((0, 13), (2, 14), (4, 18), (8, 22))),
-    ("high_spread", ((3, 19), (1, 21), (5, 23))),
-    ("low_spread", ((3, 21),)),
-    ("spread", ((0, 15), (2, 16), (4, 20))),
-    ("side_spread", ((0, 18), (2, 19), (4, 22), (3, 23))),
-    ("core_spread", ((0, 19), (2, 20), (4, 23))),
+    ("mp", ((0, 6), (2, 7), (3, 10), (4, 11), (5, 13), (6, 16), (8, 17), (9, 19), (11, 21))),
+    ("both", ((1, 7), (7, 12), (10, 16))),
+    ("side", ((0, 10), (2, 11), (3, 13), (6, 18))),
+    ("side_line", ((4, 14), (5, 17), (8, 19), (9, 21))),
+    ("then_mp", ((1, 14), (7, 19), (10, 23))),
+    ("low", ((0, 12), (2, 13), (3, 15), (1, 16), (6, 20), (7, 22))),
+    ("high", ((0, 14), (2, 15), (3, 17), (1, 18), (6, 23))),
+    ("line", ((4, 16), (5, 19), (8, 21))),
+    ("high_spread", ((0, 16), (2, 17), (3, 20), (1, 21))),
+    ("low_spread", ((0, 18), (2, 20), (3, 23))),
+    ("spread", ((4, 20), (5, 22))),
+    ("side_spread", ((0, 20), (2, 22), (4, 23))),
+    ("core_spread", ((0, 21), (2, 23))),
 )
 REST = (
-    ("low_spread", 1), ("core_spread", 3), ("high", 7), ("side_line", 11), ("core_mp", 12), ("low", 10),
-    ("spread", 8), ("high_spread", 6), ("side_spread", 1), ("low_spread", 5), ("high", 9), ("core_spread", 1),
-    ("high_spread", 7), ("mp", 12), ("side_spread", 8), ("line", 11), ("core_spread", 8), ("low_spread", 6),
-    ("high", 10), ("side_spread", 5), ("high_spread", 9), ("low_spread", 7), ("core_spread", 5), ("side_line", 12),
-    ("spread", 11), ("side_spread", 6), ("high_spread", 10), ("low_spread", 9), ("core_spread", 6), ("line", 12),
-    ("side_spread", 7), ("core_spread", 7), ("low_spread", 10), ("side_spread", 11), ("core_spread", 11),
-    ("spread", 12), ("side_spread", 9), ("core_spread", 9), ("side_spread", 10), ("core_spread", 10),
-    ("side_spread", 12), ("core_spread", 12),
+    ("side_line", 11), ("low_spread", 1), ("core_mp", 12), ("core_spread", 4), ("line", 9), ("side_spread", 5),
+    ("spread", 8), ("low", 10), ("core_spread", 5), ("high_spread", 6), ("high", 7), ("line", 11),
+    ("side_spread", 3), ("mp", 12), ("spread", 9), ("side_spread", 1), ("core_spread", 3), ("high", 10),
+    ("core_spread", 1), ("low_spread", 6), ("high_spread", 7), ("side_spread", 8), ("side_line", 12),
+    ("core_spread", 8), ("spread", 11), ("high_spread", 10), ("side_spread", 9), ("low_spread", 7),
+    ("side_spread", 6), ("line", 12), ("low_spread", 10), ("side_spread", 11), ("core_spread", 9), ("spread", 12),
+    ("core_spread", 6), ("side_spread", 7), ("side_spread", 10), ("core_spread", 7), ("side_spread", 12),
+    ("core_spread", 11), ("core_spread", 10), ("core_spread", 12),
 )
 
 
@@ -473,7 +473,8 @@
         )
 
     def grad_save(b):
-        return pltpu.make_async_copy(keep.at[b], inputs_grad.at[b], grad_sem.at[b])
+        rng = pl.ds(al(b * high, 16), high)
+        return pltpu.make_async_copy(u2s.at[rng], inputs_grad.at[rng], grad_sem.at[lax.rem(b, 2)])
 
     def mixed_save(b):
         s = lax.rem(b, 2)
@@ -726,6 +727,7 @@
         @pl.when(b >= 2)
         def _():
             mixed_save(b - 2).wait()
+            grad_save(b - 2).wait()
 
         x1 = keep[b]
         ms[s] = (x1 + dot(chid[rng, :], wo[...])[:patch] + out_shift).astype(BF16)
@@ -750,7 +752,8 @@
         n1 = (xs[s].astype(F32) - stats[b, :, 0:1]) * stats[b, :, 1:2]
         row_acc[pl.ds(0, 1), :] += jnp.sum(du1 * n1, 0, keepdims=True)
         row_acc[pl.ds(1, 1), :] += jnp.sum(du1, 0, keepdims=True)
-        keep[b] = keep[b] + norm_back(du1, n1, stats[b, :, 1:2], gain1)
+        dx = keep[b] + norm_back(du1, n1, stats[b, :, 1:2], gain1)
+        u2s[pl.ds(al(b * high, 16), patch), :] = dx.astype(BF16)
         grad_save(b).start()
         point(chunks + 2 * b + 1, range(chunks + 1, chunks + 2 * images, 2))
         return 0
@@ -780,16 +783,15 @@
         steps[name](c, half if c < chunks else last_half, STRAIGHT.index(c) if c in STRAIGHT else 0)
     for b in range(max(images - 2, 0), images):
         mixed_save(b).wait()
-    for b in range(images):
         grad_save(b).wait()
 
 
 def widen(
     sizes, summed, mixed_in, grad_in,
     mixed, inputs_grad, d_in, d_out, d_tin, d_tbias, d_tout, d_tshift, d_gain1, d_shift1, d_gain2, d_shift2, d_cbias, d_cshift,
-    sums, last, wide_in, wide_out, hold_mixed, hold_grad, in_sem, out_sem, last_sem, through_sem,
+    sums, last, wide_in, wide_out, hold_mixed, hold_grad, wide_grad, in_sem, out_sem, last_sem, through_sem,
 ):
-    images, patch, width, token_half, chunks = sizes
+    images, patch, high, width, token_half, chunks = sizes
 
     def at(c):
         return pl.ds(c * LANES, LANES)
@@ -806,16 +808,25 @@
         pltpu.make_async_copy(summed.at[m, chunks, :, pl.ds(0, last.shape[2])], last.at[m], last_sem.at[m]) for m in (0, 1)
     ]
     ins, outs = [], []
-    for i, (src, hold, dst) in enumerate(((mixed_in, hold_mixed, mixed), (grad_in, hold_grad, inputs_grad))):
-        for b in range(images):
-            ins.append(pltpu.make_async_copy(src.at[b], hold.at[b], through_sem.at[i, b]))
-            outs.append(pltpu.make_async_copy(hold.at[b], dst.at[b], through_sem.at[i + 2, b]))
+    for b in range(images):
+        ins.append(pltpu.make_async_copy(mixed_in.at[b], hold_mixed.at[b], through_sem.at[0, b]))
+        outs.append(pltpu.make_async_copy(hold_mixed.at[b], mixed.at[b], through_sem.at[2, b]))
+    for b in range(images):
+        ins.append(pltpu.make_async_copy(grad_in.at[pl.ds(b * high, high)], hold_grad.at[b], through_sem.at[1, b]))
+        outs.append(pltpu.make_async_copy(wide_grad.at[b], inputs_grad.at[b], through_sem.at[3, b]))
+
+    def pass_on(i):
+        ins[i].wait()
+        if i >= images:
+            wide_grad[i - images] = hold_grad[i - images, pl.ds(0, patch), :].astype(F32)
+        outs[i].start()
+
     for pair in loads:
         for copy in pair:
             copy.start()
     for copy in load_last + ins:
         copy.start()
-    through = iter(zip(ins, outs))
+    through = iter(range(2 * images))
     for c in range(chunks):
         for copy in loads[c]:
             copy.wait()
@@ -823,12 +834,10 @@
         stores[c][0].start()
         wide_out[c * LANES : (c + 1) * LANES, :] = sums[1, c].reshape(width, LANES).T.astype(F32)
         stores[c][1].start()
-        for arrived, leave in [pair for pair in (next(through, None),) if pair]:
-            arrived.wait()
-            leave.start()
-    for arrived, leave in through:
-        arrived.wait()
-        leave.start()
+        for i in [i for i in (next(through, None),) if i is not None]:
+            pass_on(i)
+    for i in through:
+        pass_on(i)
     for copy in load_last:
         copy.wait()
 
@@ -884,7 +893,7 @@
         functools.partial(layer, sizes),
         out_shape=(
             jax.ShapeDtypeStruct((images, patch, width), BF16),
-            jax.ShapeDtypeStruct((images, patch, width), F32),
+            jax.ShapeDtypeStruct((images * high, width), BF16),
             jax.ShapeDtypeStruct((2, n, 2, half, LANES), BF16),
             jax.ShapeDtypeStruct((images, tokens, width), BF16),
             jax.ShapeDtypeStruct((images, tokens, width), BF16),
@@ -933,7 +942,7 @@
             dma((ticks, 2)),
             dma((5, 2)),
             dma((10,)),
-            dma((images,)),
+            dma((2,)),
             dma((3,)), dma((3,)),
             dma((ticks, 4)), dma((ticks, 6)),
             dma((2, 2)), dma((2, 2)),
@@ -962,7 +971,7 @@
         mixed, inputs_grad, d_in, d_out, d_tin, d_tbias, d_tout, d_tshift,
         d_gain1, d_shift1, d_gain2, d_shift2, d_cbias, d_cshift,
     ) = pl.pallas_call(
-        functools.partial(widen, (images, patch, width, token_half, chunks)),
+        functools.partial(widen, (images, patch, high, width, token_half, chunks)),
         in_specs=[hbm] * 3,
         out_specs=(hbm,) * 4 + (vmem,) * len(shapes),
         out_shape=(
@@ -977,6 +986,7 @@
             pltpu.VMEM((width, hidden_half), F32),
             pltpu.VMEM((hidden_half, width), F32),
             pltpu.VMEM((images, patch, width), BF16),
+            pltpu.VMEM((images, high, width), BF16),
             pltpu.VMEM((images, patch, width), F32),
             dma((2, chunks)), dma((2, chunks)), dma((2,)), dma((4, images)),
         ],

time: 122 us -> 119 us (0.975)
  Pallas kernels: 121 us -> 118 us
    pallas_call x1, Pallas kernels: 10.4 us -> 9 us  [per_device(): pl.pallas_call(functools.partial(widen, (images, patch, high, width, toke...]
where the time goes in v4:
time: 119 us
  Pallas kernels  118 us (99%)
    pallas_call x1, Pallas kernels, per_device(): pl.pallas_call(functools.partial(layer, sizes), out_shape=(jax.ShapeDtype...  109 us
    pallas_call x1, Pallas kernels, per_device(): pl.pallas_call(functools.partial(widen, (images, patch, high, width, toke...  9 us

profile of v4, /device:TPU:0, one launch (start us, length us, event | category | flops | bytes accessed | tf_op | source)
XLA Modules:
  0.0 119.2 jit_solution(5034020485828535129)
XLA Ops:
  0.7 109.4 %mixer_layer.1 = (bf16[6,196,768]{2,1,0:T(8,128)(2,1)}, bf16[1248,768]{1,0:T(8,128)(2,1)}, bf16[2,13,2,384,128]{4,3,2,1,0:T(8,128)(2,1)}, bf16[6,384,768]{2,1,0:T(8,128)(2,1)}, bf16[6,384,768]{2,1,0:T(8,128)(2,1)}) custom-call(bf16[6,196,768]{2,1,0:T(8,128)(2,1)} %patches.1, bf16[6,196,768]{2,1,0:T(8,128)(2,1)} %cotangent.1, f32[768]{0:T(1024)} %gain_one.1, ...), custom_call_target="tpu_custom_call" | custom-call | tf_op jit(solution)/shard_map/mixer_layer/pallas_call | solution.py:892
  110.1 9.0 %widen.1 = (bf16[6,196,768]{2,1,0:T(8,128)(2,1)}, f32[6,196,768]{2,1,0:T(8,128)}, f32[768,1536]{1,0:T(8,128)}, f32[1536,768]{1,0:T(8,128)}, f32[192,196]{1,0:T(8...) custom-call(bf16[2,13,2,384,128]{4,3,2,1,0:T(8,128)(2,1)} %get-tuple, ...), custom_call_target="tpu_custom_call" | custom-call | tf_op jit(solution)/shard_map/widen/pallas_call | solution.py:973

commit v5 on v4

--- a/solution.py
+++ b/solution.py
@@ -793,17 +793,24 @@
 ):
     images, patch, high, width, token_half, chunks = sizes
 
-    def at(c):
-        return pl.ds(c * LANES, LANES)
-
-    loads = [[pltpu.make_async_copy(summed.at[m, c], sums.at[m, c], in_sem.at[m, c]) for m in (0, 1)] for c in range(chunks)]
-    stores = [
-        (
-            pltpu.make_async_copy(wide_in.at[:, at(c)], d_in.at[:, at(c)], out_sem.at[0, c]),
-            pltpu.make_async_copy(wide_out.at[at(c)], d_out.at[at(c)], out_sem.at[1, c]),
+    group = 3 if chunks % 3 == 0 else 1
+
+    def span(c):
+        return pl.ds(c * LANES, group * LANES)
+
+    loads = {
+        c: [
+            pltpu.make_async_copy(summed.at[m, pl.ds(c, group)], sums.at[m, pl.ds(c, group)], in_sem.at[m, c]) for m in (0, 1)
+        ]
+        for c in range(0, chunks, group)
+    }
+    stores = {
+        c: (
+            pltpu.make_async_copy(wide_in.at[:, span(c)], d_in.at[:, span(c)], out_sem.at[0, c]),
+            pltpu.make_async_copy(wide_out.at[span(c)], d_out.at[span(c)], out_sem.at[1, c]),
         )
-        for c in range(chunks)
-    ]
+        for c in range(0, chunks, group)
+    }
     load_last = [
         pltpu.make_async_copy(summed.at[m, chunks, :, pl.ds(0, last.shape[2])], last.at[m], last_sem.at[m]) for m in (0, 1)
     ]
@@ -821,19 +828,20 @@
             wide_grad[i - images] = hold_grad[i - images, pl.ds(0, patch), :].astype(F32)
         outs[i].start()
 
-    for pair in loads:
+    for pair in loads.values():
         for copy in pair:
             copy.start()
     for copy in load_last + ins:
         copy.start()
     through = iter(range(2 * images))
     for c in range(chunks):
-        for copy in loads[c]:
+        for copy in loads.get(c, ()):
             copy.wait()
         wide_in[:, c * LANES : (c + 1) * LANES] = sums[0, c].reshape(width, LANES).astype(F32)
-        stores[c][0].start()
         wide_out[c * LANES : (c + 1) * LANES, :] = sums[1, c].reshape(width, LANES).T.astype(F32)
-        stores[c][1].start()
+        if (c + 1) % group == 0:
+            for copy in stores[c + 1 - group]:
+                copy.start()
         for i in [i for i in (next(through, None),) if i is not None]:
             pass_on(i)
     for i in through:
@@ -859,7 +867,7 @@
         ref[...] = vector(v * blocks, blocks).reshape(width)
     d_tshift[...] = vector(5 * blocks, 2)[:, :patch].reshape(patch)
     d_cbias[...] = vector(5 * blocks + 2, chunks).reshape(chunks * LANES)
-    for pair in stores:
+    for pair in stores.values():
         for copy in pair:
             copy.wait()
     for copy in outs:

time: 119 us -> 119 us (level)
  no operation moved by 1% of the time
where the time goes in v5:
time: 119 us
  Pallas kernels  118 us (99%)
    pallas_call x1, Pallas kernels, per_device(): pl.pallas_call(functools.partial(layer, sizes), out_shape=(jax.ShapeDtype...  109 us
    pallas_call x1, Pallas kernels, per_device(): pl.pallas_call(functools.partial(widen, (images, patch, high, width, toke...  8.81 us

profile of v5, /device:TPU:0, one launch (start us, length us, event | category | flops | bytes accessed | tf_op | source)
XLA Modules:
  0.0 119.0 jit_solution(8880807368147904238)
XLA Ops:
  0.7 109.4 %mixer_layer.1 = (bf16[6,196,768]{2,1,0:T(8,128)(2,1)}, bf16[1248,768]{1,0:T(8,128)(2,1)}, bf16[2,13,2,384,128]{4,3,2,1,0:T(8,128)(2,1)}, bf16[6,384,768]{2,1,0:T(8,128)(2,1)}, bf16[6,384,768]{2,1,0:T(8,128)(2,1)}) custom-call(bf16[6,196,768]{2,1,0:T(8,128)(2,1)} %patches.1, bf16[6,196,768]{2,1,0:T(8,128)(2,1)} %cotangent.1, f32[768]{0:T(1024)} %gain_one.1, ...), custom_call_target="tpu_custom_call" | custom-call | tf_op jit(solution)/shard_map/mixer_layer/pallas_call | solution.py:900
  110.1 8.8 %widen.1 = (bf16[6,196,768]{2,1,0:T(8,128)(2,1)}, f32[6,196,768]{2,1,0:T(8,128)}, f32[768,1536]{1,0:T(8,128)}, f32[1536,768]{1,0:T(8,128)}, f32[192,196]{1,0:T(8...) custom-call(bf16[2,13,2,384,128]{4,3,2,1,0:T(8,128)(2,1)} %get-tuple, ...), custom_call_target="tpu_custom_call" | custom-call | tf_op jit(solution)/shard_map/widen/pallas_call | solution.py:981

commit v6 on v5

--- a/solution.py
+++ b/solution.py
@@ -66,8 +66,12 @@
     )
 
 
+def phi_of(v):
+    return 0.5 + 0.5 * lax.erf(v * 0.7071067811865476)
+
+
 def gelu_parts(v):
-    phi = 0.5 + 0.5 * lax.erf(v * 0.7071067811865476)
+    phi = phi_of(v)
     return phi, phi + v * (0.3989422804014327 * jnp.exp(-0.5 * v * v))
 
 
@@ -75,10 +79,10 @@
     sizes,
     patches, cotangent, gain_one, shift_one, token_in, token_bias, token_out, token_shift,
     gain_two, shift_two, channel_in, channel_bias, channel_out, channel_shift,
-    mixed, inputs_grad, summed, hid_out, slope_out,
+    mixed, inputs_grad, summed, hid_out, before_out,
     wi, wo, vecs, cbs, cbo, tbs, tss, tins, touts, tw, twi_t, two_t, keep,
     dys, dys_t, u2s, u2s_t, u1s, chid, dcp, dtok,
-    xs, ms, hid, slope, stats,
+    xs, ms, hid, before, stats,
     row_acc, cb_acc, tin_acc, tout_acc, small,
     grads, from_core, acc, from_mp, from_x, from_z, from_far,
     load_sem, stage_sem, small_sem, grad_sem, tok_s, tok_r, w_s, w_r, wc_s, wc_r, c_s, c_r, g_s, line_s, l_sem, y_r, x_r, z_r, zh_r, zl_r,
@@ -462,14 +466,14 @@
         s = lax.rem(b, 2)
         return (
             pltpu.make_async_copy(hid.at[s, pl.ds(0, 2 * token_half)], hid_out.at[b], stage_sem.at[2, s]),
-            pltpu.make_async_copy(slope.at[s], slope_out.at[b], stage_sem.at[3, s]),
+            pltpu.make_async_copy(before.at[s], before_out.at[b], stage_sem.at[3, s]),
         )
 
     def hid_load(b):
         s = lax.rem(b, 2)
         return (
             pltpu.make_async_copy(hid_out.at[b], hid.at[s, pl.ds(0, 2 * token_half)], stage_sem.at[2, s]),
-            pltpu.make_async_copy(slope_out.at[b], slope.at[s], stage_sem.at[3, s]),
+            pltpu.make_async_copy(before_out.at[b], before.at[s], stage_sem.at[3, s]),
         )
 
     def grad_save(b):
@@ -575,10 +579,9 @@
         stats[b, :, 1:2] = scale
         u1s[b, pl.ds(0, patch), :] = (centred * scale * gain1 + shift1).astype(BF16)
         pre = dot(twi[pl.ds(0, token_half), pl.ds(0, high)], u1s[b])
-        phi, deriv = gelu_parts(pre)
         at = pl.ds(al(b * token_half, 16), token_half)
-        chid[at, pl.ds(0, width)] = (pre * phi).astype(BF16)
-        dcp[at, pl.ds(0, width)] = deriv.astype(BF16)
+        chid[at, pl.ds(0, width)] = (pre * phi_of(pre)).astype(BF16)
+        dcp[at, pl.ds(0, width)] = pre.astype(BF16)
         cot_copy(b).wait()
         value = ms[s]
 
@@ -617,7 +620,6 @@
     def token_forward(b, _):
         s = lax.rem(b, 2)
         pre = dot(twi[pl.ds(token_half, token_half), pl.ds(0, high)], u1s[b])
-        phi, deriv = gelu_parts(pre)
 
         @pl.when(b >= 2)
         def _():
@@ -625,9 +627,9 @@
 
         at = pl.ds(al(b * token_half, 16), token_half)
         hid[s, pl.ds(0, token_half), :] = chid[at, pl.ds(0, width)]
-        slope[s, pl.ds(0, token_half), :] = dcp[at, pl.ds(0, width)]
-        hid[s, pl.ds(token_half, token_half), :] = (pre * phi).astype(BF16)
-        slope[s, pl.ds(token_half, token_half), :] = deriv.astype(BF16)
+        before[s, pl.ds(0, token_half), :] = dcp[at, pl.ds(0, width)]
+        hid[s, pl.ds(token_half, token_half), :] = (pre * phi_of(pre)).astype(BF16)
+        before[s, pl.ds(token_half, token_half), :] = pre.astype(BF16)
         both(hid_save(b), "start")
         x1 = keep[b] + dot(two_t[pl.ds(0, high), :], hid[s])[:patch]
         keep[b] = x1
@@ -745,7 +747,7 @@
         dtk = dtok[...]
         hidden = hid[s]
         tout_acc[:, pl.ds(0, high)] += dot_nt(hidden, dtk)
-        dpre = (dot(two[pl.ds(0, tokens), pl.ds(0, high)], dtk) * slope[s].astype(F32)).astype(BF16)
+        dpre = (dot(two[pl.ds(0, tokens), pl.ds(0, high)], dtk) * gelu_parts(before[s].astype(F32))[1]).astype(BF16)
         tin_acc[:, pl.ds(0, high)] += dot_nt(dpre, u1s[b])
         du1 = dot(twi_t[pl.ds(0, high), :], dpre)[:patch]
         patch_copy(b).wait()

time: 119 us -> 119 us (level)
  no operation moved by 1% of the time
where the time goes in v6:
time: 119 us
  Pallas kernels  118 us (99%)
    pallas_call x1, Pallas kernels, per_device(): pl.pallas_call(functools.partial(layer, sizes), out_shape=(jax.ShapeDtype...  109 us
    pallas_call x1, Pallas kernels, per_device(): pl.pallas_call(functools.partial(widen, (images, patch, high, width, toke...  8.81 us

profile of v6, /device:TPU:0, one launch (start us, length us, event | category | flops | bytes accessed | tf_op | source)
XLA Modules:
  0.0 118.7 jit_solution(3305445836482484066)
XLA Ops:
  0.7 109.1 %mixer_layer.1 = (bf16[6,196,768]{2,1,0:T(8,128)(2,1)}, bf16[1248,768]{1,0:T(8,128)(2,1)}, bf16[2,13,2,384,128]{4,3,2,1,0:T(8,128)(2,1)}, bf16[6,384,768]{2,1,0:T(8,128)(2,1)}, bf16[6,384,768]{2,1,0:T(8,128)(2,1)}) custom-call(bf16[6,196,768]{2,1,0:T(8,128)(2,1)} %patches.1, bf16[6,196,768]{2,1,0:T(8,128)(2,1)} %cotangent.1, f32[768]{0:T(1024)} %gain_one.1, ...), custom_call_target="tpu_custom_call" | custom-call | tf_op jit(solution)/shard_map/mixer_layer/pallas_call | solution.py:902
  109.8 8.8 %widen.1 = (bf16[6,196,768]{2,1,0:T(8,128)(2,1)}, f32[6,196,768]{2,1,0:T(8,128)}, f32[768,1536]{1,0:T(8,128)}, f32[1536,768]{1,0:T(8,128)}, f32[192,196]{1,0:T(8...) custom-call(bf16[2,13,2,384,128]{4,3,2,1,0:T(8,128)(2,1)} %get-tuple, ...), custom_call_target="tpu_custom_call" | custom-call | tf_op jit(solution)/shard_map/widen/pallas_call | solution.py:983
